TPU v7x, 32 devices: a whole 2x2x4 slice. The times are simulated.
32 devices in a mesh: parts: 2 (over x), lon: 16 (over z, y, core).
Axes of the slice: x: 2, y: 2, z: 4, core: 2. Of those that a mesh axis runs over, the one named last changes fastest.
Arguments:
- cotangent: float32 [96, 2048, 256], P(None, ('parts', 'lon')), parts along dimension 1, may hold values from -6 to 6
- synthesis: float32 [96, 96], replicated, may hold values from -0.625 to 0.625
- analysis: float32 [96, 96], replicated, may hold values from -0.625 to 0.625
- depths: float32 [96], replicated, may hold values from 0.2 to 5
- metric: float32 [1024, 256], P('lon'), may hold values from 0.5 to 2
- east_face: float32 [1024, 256], P('lon'), may hold values from 0.1 to 1
- north_face: float32 [1024, 256], P('lon'), may hold values from 0.1 to 1
Outputs:
- right_cotangent: float32 [96, 2048, 256], P(None, ('parts', 'lon')), parts along dimension 1
There are 2 independent parts, one for each index of `parts`. A program takes and returns all parts, laid end to end along the dimension named above; an argument that names none is the same for every part. Nothing has to cross between parts.
All inputs are finite; a program needn't handle non-finite values.
Results may differ from a plain program's by a relative error of at most 0.000073.
Values sent between devices are 32-bit elements; how exact they have to be, the bound alone decides.
No kernel may reach another device: no remote copies, remote signals or barrier semaphores. Data moves between devices by JAX's collectives and lax.ppermute only.
A program may use at most 192 MiB of HBM per device.

v0:
```python
import functools
import math

import jax
import jax.numpy as jnp
from jax import lax
from jax.experimental import pallas as pl
from jax.experimental.pallas import tpu as pltpu
from jax.sharding import PartitionSpec as P

G = 16
H = 128
VMEM_LIMIT = 56 * 1024 * 1024
COS1, COS2 = math.cos(2 * math.pi / 5), math.cos(4 * math.pi / 5)
SIN1, SIN2 = math.sin(2 * math.pi / 5) ** 2, math.sin(4 * math.pi / 5) ** 2


def column(row):
    n = row.shape[1]
    eye = lax.broadcasted_iota(jnp.int32, (n, n), 0) == lax.broadcasted_iota(jnp.int32, (n, n), 1)
    picked = jnp.sum(jnp.where(eye, jnp.broadcast_to(row, (n, n)), 0.0), axis=1, keepdims=True)
    return jnp.broadcast_to(picked, (n, H))


def split(x):
    high = x.astype(jnp.bfloat16)
    low = (x - high.astype(jnp.float32)).astype(jnp.bfloat16)
    return high, low


def prepare(depths_ref, syn_ref, ana_ref, cols_ref, ws_ref, wa_ref):
    row = depths_ref[...]
    centre = 1.25 * row + 4.0
    half = 0.75 * row + 4.0
    product = row * (row + 4.0)
    c2, h2 = centre * centre, half * half
    gain = 16.0 / (centre * (16.0 * c2 * c2 - 20.0 * c2 * h2 + 5.0 * h2 * h2))
    d = column(row)
    cols_ref[0] = d
    cols_ref[1] = (1.0 - COS1) * (1.25 * d + 4.0)
    cols_ref[2] = (1.0 - COS2) * (1.25 * d + 4.0)
    cols_ref[3] = SIN1 * (d * (d + 4.0))
    cols_ref[4] = SIN2 * (d * (d + 4.0))
    n = row.shape[1]
    for src, dst, scale in ((syn_ref[...].T, ws_ref, None), (ana_ref[...].T, wa_ref, gain)):
        if scale is not None:
            src = src * scale
        high, low = split(src)
        dst[:, :n] = high
        dst[:, n : 2 * n] = high
        dst[:, 2 * n :] = low


def mix(weights, field):
    high, low = split(field)
    stacked = jnp.concatenate([high, low, high], axis=0)
    return jnp.dot(weights, stacked, preferred_element_type=jnp.float32)


def halves(ref, slot, rows):
    return ref[slot, rows, :H], ref[slot, rows, H:]


def put(ref, slot, rows, pair):
    ref[slot, rows, :H] = pair[0]
    ref[slot, rows, H:] = pair[1]


def coefficients(co_ref, k):
    e = co_ref[0, pl.ds(k, 1), :]
    w = co_ref[0, pl.ds(k - 1, 1), :]
    n = co_ref[1, pl.ds(k, 1), :]
    s = co_ref[2, pl.ds(k, 1), :]
    return tuple((c[:, :H], c[:, H:]) for c in (e, w, n, s))


def operate(diag, y, east, west, co):
    lanes = lax.broadcasted_iota(jnp.int32, (G, H), 1)
    (ea, eb), (wa, wb), (na, nb), (sa, sb) = co
    ya, yb = y
    na_r, nb_r = pltpu.roll(ya, H - 1, 1), pltpu.roll(yb, H - 1, 1)
    sa_r, sb_r = pltpu.roll(ya, 1, 1), pltpu.roll(yb, 1, 1)
    na_r = jnp.where(lanes == H - 1, nb_r, na_r)
    sb_r = jnp.where(lanes == 0, sa_r, sb_r)
    a = (diag[0] * ya - ea * east[0]) - (wa * west[0] + na * na_r + sa * sa_r)
    b = (diag[1] * yb - eb * east[1]) - (wb * west[1] + nb * nb_r + sb * sb_r)
    return a, b


def fill_coefficients(co_ref, at, metric, east, north):
    rows = metric.shape[0]
    lanes = lax.broadcasted_iota(jnp.int32, (rows, H), 1)
    na, nb = north[:, :H], north[:, H:]
    sa, sb = pltpu.roll(na, 1, 1), pltpu.roll(nb, 1, 1)
    sb = jnp.where(lanes == 0, sa, sb)
    sa = jnp.where(lanes == 0, 0.0, sa)
    here = pl.ds(at, rows)
    co_ref[0, here, :] = east
    co_ref[1, here, :H] = na
    co_ref[1, here, H:] = jnp.where(lanes == H - 1, 0.0, nb)
    co_ref[2, here, :H] = sa
    co_ref[2, here, H:] = sb
    co_ref[3, here, :] = metric
    west = co_ref[0, pl.ds(at - 1, rows), :]
    faces = east + west + north
    co_ref[4, here, :H] = faces[:, :H] + sa
    co_ref[4, here, H:] = faces[:, H:] + sb


def diagonals(cols_ref, co_ref, k, rows):
    m, f = co_ref[3, pl.ds(k, 1), :], co_ref[4, pl.ds(k, 1), :]
    d, a1, a2 = cols_ref[0, rows, :], cols_ref[1, rows, :], cols_ref[2, rows, :]
    ta, tb = d * m[:, :H] + f[:, :H], d * m[:, H:] + f[:, H:]
    return (ta - a1, tb - a1), (ta - a2, tb - a2)


def groups(levels):
    return [pl.ds(g * G, G) for g in range(levels // G)]


def step1(levels, cols, co, k, r, r_e, r_w, store, d1, d2):
    c = coefficients(co, k)
    for rows in groups(levels):
        first, second = diagonals(cols, co, k, rows)
        put(*d1, rows, first)
        put(*d2, rows, second)
        put(*store, rows, operate(first, halves(*r, rows), halves(*r_e, rows), halves(*r_w, rows), c))


def step_even(levels, cols, which, co, k, y, y_e, y_w, old, diag, store):
    c = coefficients(co, k)
    for rows in groups(levels):
        a, b = operate(halves(*diag, rows), halves(*y, rows), halves(*y_e, rows), halves(*y_w, rows), c)
        beta = cols[which, rows, :]
        oa, ob = halves(*old, rows)
        store(rows, (a + beta * oa, b + beta * ob))


def step3(levels, co, k, y, y_e, y_w, diag, store):
    c = coefficients(co, k)
    for rows in groups(levels):
        put(*store, rows, operate(halves(*diag, rows), halves(*y, rows), halves(*y_e, rows), halves(*y_w, rows), c))


def start(copies):
    for copy in copies:
        copy.start()


def wait(copies):
    for copy in copies:
        copy.wait()


def load_row(flat, block, j, levels):
    at = block * (2 * levels * 8) + j
    return jnp.concatenate([flat[pl.ds(at + h * levels * 8, levels, stride=8), :] for h in range(2)], axis=1)


def store_row(flat, block, j, levels, value):
    at = block * (2 * levels * 8) + j
    for h in range(2):
        flat[pl.ds(at + h * levels * 8, levels, stride=8), :] = value[:, h * H : (h + 1) * H]


def interior(first, last, t0, t1, levels, lon, *refs):
    refs = list(refs)
    take = lambda n: [refs.pop(0) for _ in range(n)]
    x_ref, metric_ref, east_ref, north_ref = take(4)
    if first:
        dep_ref, syn_ref, ana_ref = take(3)
    else:
        cols, ws, wa, r0, u0, y0, w0, e0, g0, _out_in = take(10)
    out_ref, edge_ref, save_ref = take(3)
    if first:
        cols, ws, wa = take(3)
    if not last:
        state = take(6)
    co, cbuf, obuf, zbuf, rr, uu, yy, ww, d1, d2, in_sem, out_sem = take(12)
    assert not refs

    blocks = lon // 8
    b_in0 = 0 if first else t0 // 2
    b_in1 = blocks if last else t1 // 2 + 1
    b_in1 = min(b_in1, blocks)

    def fetch(b):
        return [
            pltpu.make_async_copy(x_ref.at[:, pl.ds(8 * b, 8), pl.ds(h * H, H)], cbuf.at[b - b_in0, h], in_sem.at[h, b - b_in0])
            for h in range(2)
        ]

    b_out0 = 1 if first else (t0 - 1) // 2
    b_out1 = blocks - 1 if last else (t1 - 1) // 2

    def flush(b):
        return [
            pltpu.make_async_copy(
                obuf.at[b - (b_out0 - 1), h], out_ref.at[:, pl.ds(8 * b, 8), pl.ds(h * H, H)], out_sem.at[h, b - b_out0])
            for h in range(2)
        ]

    for b in range(b_in0, b_in1):
        start(fetch(b))

    co[0, pl.ds(0, 8), :] = jnp.zeros((8, 2 * H), jnp.float32)
    fill_coefficients(co, 8, metric_ref[...], east_ref[...], north_ref[...])
    if first:
        prepare(dep_ref, syn_ref, ana_ref, cols, ws, wa)
    else:
        for src, dst in ((r0, rr), (u0, uu), (y0, yy), (w0, ww), (e0, d1), (g0, d2)):
            dst[...] = src[...]

    rows_in = cbuf.reshape(cbuf.shape[0] * 2 * levels * 8, H)
    rows_out = obuf.reshape(obuf.shape[0] * 2 * levels * 8, H)

    wait(fetch(b_in0))
    if first:
        rr[0] = mix(ws[...], load_row(rows_in, 0, 0, levels))
        save_ref[0, 0] = rr[0]

    def finish(row):
        o = jnp.dot(wa[...], zbuf[...], preferred_element_type=jnp.float32)
        b = lax.div(row + 8, 8) - 1 - (b_out0 - 1)
        store_row(rows_out, b, lax.rem(row + 8, 8), levels, o)

    def store_z(rows, pair):
        start = rows.start
        for h in range(2):
            high, low = split(pair[h])
            lanes = slice(h * H, (h + 1) * H)
            zbuf[pl.ds(start, G), lanes] = high
            zbuf[pl.ds(levels + start, G), lanes] = low
            zbuf[pl.ds(2 * levels + start, G), lanes] = high

    def body(t, _):
        b = lax.div(t + 1, 2)

        @pl.when((lax.rem(t, 2) == 1) & (b < b_in1) & (b > b_in0))
        def _():
            wait(fetch(b))

        for s in range(4):
            i = 4 * t + s
            nxt = i + 1
            bb = lax.div(nxt, 8) - b_in0
            finish_row = i - 5
            if first:
                finish_row = jnp.maximum(finish_row, 0)
            finish(finish_row)
            rr[(s + 1) % 4] = mix(ws[...], load_row(rows_in, bb, lax.rem(nxt, 8), levels))
            k = 8 + i
            q = lambda n: (s + n) % 4
            step1(levels, cols, co, k - 1, (rr, q(3)), (rr, q(0)), (rr, q(2)), (uu, q(3)), (d1, q(3)), (d2, q(3)))
            step_even(levels, cols, 3, co, k - 2, (uu, q(2)), (uu, q(3)), (uu, q(1)), (rr, q(2)), (d1, q(2)),
                      lambda rows, pair, at=q(2): put(yy, at, rows, pair))
            step3(levels, co, k - 3, (yy, q(1)), (yy, q(2)), (yy, q(0)), (d2, q(1)), (ww, q(1)))
            step_even(levels, cols, 4, co, k - 4, (ww, q(0)), (ww, q(1)), (ww, q(3)), (yy, q(0)), (d2, q(0)), store_z)

        if first:

            @pl.when(t == 0)
            def _():
                save_ref[0, 1] = rr[1]
                save_ref[1, 0] = uu[1]
                save_ref[1, 1] = uu[2]

            @pl.when(t == 1)
            def _():
                save_ref[2, 0] = yy[2]
                save_ref[2, 1] = yy[3]
                save_ref[3, 0] = ww[3]
                save_ref[3, 1] = ww[0]

        bo = lax.div(t - 3, 2)

        @pl.when((lax.rem(t, 2) == 1) & (t >= 3) & (bo >= b_out0) & (bo < b_out1))
        def _():
            start(flush(bo))

        return 0

    lax.fori_loop(t0, t1, body, 0)
    finish(jnp.int32(4 * t1 - 5))
    if not last:
        start(flush(b_out1 - 1))
        for src, dst in zip((rr, uu, yy, ww, d1, d2), state):
            dst[...] = src[...]
    if first:
        edge_ref[...] = obuf[0]
    else:
        edge_ref[...] = obuf[blocks - 1 - (b_out0 - 1)]
    if last:
        at = 4 * t1
        for f, (ref, row) in enumerate(((rr, at - 2), (uu, at - 3), (yy, at - 4), (ww, at - 5))):
            save_ref[f, 0] = ref[row % 4]
            save_ref[f, 1] = ref[(row + 1) % 4]
    for b in range(b_out0, b_out1):
        wait(flush(b))


def edges(levels, lon, *refs):
    (hl, hr, metric_ref, east_ref, north_ref, cols, ws, wa, save_l, save_r, edge_l, edge_r, _out_in,
     out_ref, co, rr, uu, yy, ww, d1, d2, zbuf, obuf, sems) = refs
    copies = []
    for side in range(2):
        halo = hr if side else hl
        c = co.at[side]
        c[0, pl.ds(0, 8), :] = jnp.zeros((8, 2 * H), jnp.float32)
        own = pl.ds(lon - 8, 8) if side else pl.ds(0, 8)
        mine = (metric_ref[own, :], east_ref[own, :], north_ref[own, :])
        theirs = [halo[:, levels + f, :] for f in range(3)]
        if side:
            window = [jnp.concatenate([a, b], axis=0) for a, b in zip(mine, theirs)]
            base = 8 + 4
        else:
            window = [jnp.concatenate([b, a], axis=0) for a, b in zip(mine, theirs)]
            base = 8
        fill_coefficients(c, 8, *window)
        r, u, y, w = rr.at[side], uu.at[side], yy.at[side], ww.at[side]
        e, g = d1.at[side], d2.at[side]
        save = save_r if side else save_l
        edge = edge_r if side else edge_l
        new_r = 4 if side else 0
        for j in range(4):
            r[new_r + j] = mix(ws[...], halo[j, :levels, :])
        u0, y0, w0, z0 = (3, 2, 1, 0) if side else (1, 2, 3, 4)
        old_r, old_u, old_y, old_w = (2, 1, 0, -1) if side else (4, 5, 6, 7)
        for f, (ref, row) in enumerate(((r, old_r), (u, old_u), (y, old_y), (w, old_w + 1))):
            ref[row] = save[f, 0]
            ref[row + 1] = save[f, 1]
        for n in range(0, 4) if side else range(4, 8):
            if not (u0 <= n < u0 + 4):
                for rows in groups(levels):
                    first, second = diagonals(cols, c, base + n, rows)
                    put(e, n, rows, first)
                    put(g, n, rows, second)
        for j in range(4):
            n = u0 + j
            step1(levels, cols, c, base + n, (r, n), (r, n + 1), (r, n - 1), (u, n), (e, n), (g, n))
        for j in range(4):
            n = y0 + j
            step_even(levels, cols, 3, c, base + n, (u, n), (u, n + 1), (u, n - 1), (r, n), (e, n),
                      lambda rows, pair, n=n: put(y, n, rows, pair))
        for j in range(4):
            n = w0 + j
            step3(levels, c, base + n, (y, n), (y, n + 1), (y, n - 1), (g, n), (w, n + 1))
        ob = obuf.at[side]
        ob[...] = edge[...]
        flat = ob.reshape(2 * levels * 8, H)
        for j in range(4):
            n = z0 + j
            z = zbuf.at[side, j]

            def store_z(rows, pair, z=z):
                start = rows.start
                for h in range(2):
                    high, low = split(pair[h])
                    lanes = slice(h * H, (h + 1) * H)
                    z[pl.ds(start, G), lanes] = high
                    z[pl.ds(levels + start, G), lanes] = low
                    z[pl.ds(2 * levels + start, G), lanes] = high

            step_even(levels, cols, 4, c, base + n, (w, n + 1), (w, n + 2), (w, n), (y, n), (g, n), store_z)
            o = jnp.dot(wa[...], z[...], preferred_element_type=jnp.float32)
            store_row(flat, 0, (4 + j) if side else j, levels, o)
        at = lon - 8 if side else 0
        for h in range(2):
            copies.append(pltpu.make_async_copy(ob.at[h], out_ref.at[:, pl.ds(at, 8), pl.ds(h * H, H)], sems.at[side, h]))
        start(copies[-2:])
    wait(copies)


F32, BF16 = jnp.float32, jnp.bfloat16
ANY = pl.BlockSpec(memory_space=pl.ANY)
VM = pl.BlockSpec(memory_space=pltpu.VMEM)


def shape(*dims, dtype=F32):
    return jax.ShapeDtypeStruct(dims, dtype)


def run_interior(first, last, t0, t1, levels, lon, lat, args, state, out_prev):
    ring = lambda: pltpu.VMEM((4, levels, lat), F32)
    outs = [(shape(levels, lon, lat), ANY), (shape(2, levels, 8, H), VM), (shape(4, 2, levels, lat), VM)]
    if first:
        outs += [(shape(5, levels, H), VM), (shape(levels, 3 * levels, dtype=BF16), VM), (shape(levels, 3 * levels, dtype=BF16), VM)]
    if not last:
        outs += [(shape(4, levels, lat), VM)] * 6
    blocks = lon // 8
    operands = list(args) + list(state)
    specs = [ANY] + [VM] * (len(operands) - 1)
    aliases = {}
    if out_prev is not None:
        aliases[len(operands)] = 0
        operands.append(out_prev)
        specs.append(ANY)
    return pl.pallas_call(
        functools.partial(interior, first, last, t0, t1, levels, lon),
        out_shape=[o for o, _ in outs],
        in_specs=specs,
        out_specs=[s for _, s in outs],
        input_output_aliases=aliases,
        scratch_shapes=[
            pltpu.VMEM((5, lon + 8, lat), F32),
            pltpu.VMEM((blocks + 1, 2, levels, 8, H), F32),
            pltpu.VMEM((blocks + 1, 2, levels, 8, H), F32),
            pltpu.VMEM((3 * levels, lat), BF16),
            ring(), ring(), ring(), ring(), ring(), ring(),
            pltpu.SemaphoreType.DMA((2, blocks + 1)),
            pltpu.SemaphoreType.DMA((2, blocks + 1)),
        ],
        compiler_params=pltpu.CompilerParams(vmem_limit_bytes=VMEM_LIMIT),
        name="interior",
    )(*operands)


def run_edges(levels, lon, lat, operands):
    return pl.pallas_call(
        functools.partial(edges, levels, lon),
        out_shape=shape(levels, lon, lat),
        in_specs=[VM] * 12 + [ANY],
        out_specs=ANY,
        input_output_aliases={12: 0},
        scratch_shapes=[
            pltpu.VMEM((2, 5, 24, lat), F32),
            pltpu.VMEM((2, 8, levels, lat), F32),
            pltpu.VMEM((2, 8, levels, lat), F32),
            pltpu.VMEM((2, 8, levels, lat), F32),
            pltpu.VMEM((2, 10, levels, lat), F32),
            pltpu.VMEM((2, 8, levels, lat), F32),
            pltpu.VMEM((2, 8, levels, lat), F32),
            pltpu.VMEM((2, 4, 3 * levels, lat), BF16),
            pltpu.VMEM((2, 2, levels, 8, H), F32),
            pltpu.SemaphoreType.DMA((2, 2)),
        ],
        compiler_params=pltpu.CompilerParams(vmem_limit_bytes=VMEM_LIMIT),
        name="edges",
    )(*operands)


def message(x, coeffs, lo, hi):
    return jnp.concatenate([x[:, lo:hi, :].transpose(1, 0, 2), jnp.stack([c[lo:hi] for c in coeffs], axis=1)], axis=1)


def shards(cotangent, synthesis, analysis, depths, metric, east_face, north_face):
    levels, lon, lat = cotangent.shape
    coeffs = (metric, east_face, north_face)
    count = lax.axis_size("lon")
    from_west = lax.ppermute(message(cotangent, coeffs, lon - 4, lon), "lon", [(i, (i + 1) % count) for i in range(count)])
    from_east = lax.ppermute(message(cotangent, coeffs, 0, 4), "lon", [((i + 1) % count, i) for i in range(count)])
    args = (cotangent,) + coeffs
    out, edge_l, save_l, cols, ws, wa, *state = run_interior(
        True, False, 0, 7, levels, lon, lat, args + (depths.reshape(1, -1), synthesis, analysis), (), None)
    out, edge_r, save_r = run_interior(False, True, 7, lon // 4, levels, lon, lat, args, (cols, ws, wa, *state), out)
    return run_edges(levels, lon, lat, (from_west, from_east) + coeffs + (cols, ws, wa, save_l, save_r, edge_l, edge_r, out))


def solution(mesh):
    placed = (P(None, ("parts", "lon"), None), P(), P(), P(), P("lon", None), P("lon", None), P("lon", None))
    return jax.shard_map(
        shards, mesh=mesh, in_specs=placed, out_specs=P(None, ("parts", "lon"), None), check_vma=False)
```

profile of v0, /device:TPU:0, one launch (start us, length us, event | category | flops | bytes accessed | tf_op | source)
XLA Modules:
  0.0 45.6 jit_solution(13975116959394782849)
XLA Ops:
  0.0 1.5 %fusion = (f32[96,4,256]{2,1,0:T(4,128)S(1)}, f32[96,4,256]{2,1,0:T(4,128)S(1)}) fusion(f32[96,64,256]{2,1,0:T(8,128)} %refs_0_.3), kind=kLoop, calls=%fused_computation.4 | loop fusion | bytes 1572864 | tf_op jit(solution)/shard_map/slice | solution.py:443
  1.5 0.1 copy.17
  1.6 0.7 %fusion.1 = (f32[4,256]{1,0:T(4,128)S(1)}, f32[4,256]{1,0:T(4,128)S(1)}) fusion(f32[64,256]{1,0:T(8,128)} %refs_2_.5), kind=kLoop, calls=%fused_computation.5 | loop fusion | bytes 16384 | tf_op jit(solution)/shard_map/slice | solution.py:443
  2.3 0.7 %fusion.2 = (f32[4,256]{1,0:T(4,128)S(1)}, f32[4,256]{1,0:T(4,128)S(1)}) fusion(f32[64,256]{1,0:T(8,128)} %refs_3_.5), kind=kLoop, calls=%fused_computation.6 | loop fusion | bytes 16384 | tf_op jit(solution)/shard_map/slice | solution.py:443
  3.1 0.7 %fusion.3 = (f32[4,256]{1,0:T(4,128)S(1)}, f32[4,256]{1,0:T(4,128)S(1)}) fusion(f32[64,256]{1,0:T(8,128)} %refs_4_.1), kind=kLoop, calls=%fused_computation.7 | loop fusion | bytes 16384 | tf_op jit(solution)/shard_map/slice | solution.py:443
  3.8 0.5 %collective-permute-start = (f32[4,99,256]{2,1,0:T(8,128)S(1)}, f32[4,99,256]{2,1,0:T(8,128)S(1)}, u32[]{:S(2)}, u32[]{:S(2)}) collective-permute-start(f32[4,99,256]{2,1,0:T(8,128)S(1)} %pad_maximum_fusion), channel_id=1, source_target_pairs={{0,1},{1,2},{2,3},{3,4},{4,5},{5,6},{6,7},{7,8},{8,9},{9,10},{10,1... | collective-permute-start | bytes 1216520 | tf_op jit(solution)/shard_map/ppermute | solution.py:450
  4.3 0.1 copy.16
  4.5 5.1 %collective-permute-start.1 = (f32[4,99,256]{2,1,0:T(8,128)S(1)}, f32[4,99,256]{2,1,0:T(8,128)S(1)}, u32[]{:S(2)}, u32[]{:S(2)}) collective-permute-start(f32[4,99,256]{2,1,0:T(8,128)S(1)} %pad_maximum_fusion.1), channel_id=1, source_target_pairs={{1,0},{2,1},{3,2},{4,3},{5,4},{6,5},{7,6},{8,7},{9,8},{10,9},{11,1... | collective-permute-start | bytes 1216520 | tf_op jit(solution)/shard_map/ppermute | solution.py:451
  9.6 13.6 %interior.2 = (f32[96,64,256]{2,1,0:T(8,128)}, f32[2,96,8,128]{3,2,1,0:T(8,128)}, f32[4,2,96,256]{3,2,1,0:T(8,128)}, f32[5,96,128]{2,1,0:T(8,128)}, bf16[96,288]...) custom-call(f32[96,64,256]{2,1,0:T(8,128)} %refs_0_.3, ...), custom_call_target="tpu_custom_call" | custom-call | tf_op jit(solution)/shard_map/interior/pallas_call | solution.py:398
  23.2 15.4 %interior.3 = (f32[96,64,256]{2,1,0:T(8,128)}, f32[2,96,8,128]{3,2,1,0:T(8,128)}, f32[4,2,96,256]{3,2,1,0:T(8,128)}) custom-call(f32[96,64,256]{2,1,0:T(8,128)} %refs_0_.3, f32[64,256]{1,0:T(8,128)} %refs_2_.5, f32[64,256]{1,0:T(8,128)} %refs_3_.5, f32[64,256]{1,0:T(8,128)} %refs_4_.1, ...), custom_call_target="tpu_custom_call", output_to_operand_aliasing={{0}: (13, {})} | custom-call | tf_op jit(solution)/shard_map/interior/pallas_call | solution.py:398
  38.6 0.0 collective-permute-done.refs_0_
  38.6 0.0 copy-start
  38.6 0.0 collective-permute-done.1.refs_1_
  38.6 0.0 copy-start.1
  38.6 0.7 %copy-done = f32[4,99,256]{2,1,0:T(8,128)} copy-done((f32[4,99,256]{2,1,0:T(8,128)}, f32[4,99,256]{2,1,0:T(8,128)S(1)}, u32[]{:S(2)}) %copy-start) | copy-done | bytes 405528
  39.4 0.2 copy-done.1
  39.5 6.1 %edges.1 = f32[96,64,256]{2,1,0:T(8,128)} custom-call(f32[4,99,256]{2,1,0:T(8,128)} %copy-done, f32[4,99,256]{2,1,0:T(8,128)} %copy-done.1, f32[64,256]{1,0:T(8,128)} %refs_2_.5, f32[64,256]{1,0:T(8,128)} %refs_3_.5, f32[64,256]{1,0:T(8,128)} %refs_4_.1, f32[5,96,128]{2,1,0:T(8,128)} %get-tuple-element.20.refs_4_.refs_5_, ...), custom_call_target="tpu_custom_call", output_to_operand_aliasing={{}: (12, {})} | custom-call | tf_op jit(solution)/shard_map/edges/pallas_call | solution.py:419
  (8 shorter events, 0.1 us)
Async XLA Ops:
  3.8 34.8 %collective-permute-start = (f32[4,99,256]{2,1,0:T(8,128)S(1)}, f32[4,99,256]{2,1,0:T(8,128)S(1)}, u32[]{:S(2)}, u32[]{:S(2)}) collective-permute-start(f32[4,99,256]{2,1,0:T(8,128)S(1)} %pad_maximum_fusion), channel_id=1, source_target_pairs={{0,1},{1,2},{2,3},{3,4},{4,5},{5,6},{6,7},{7,8},{8,9},{9,10},{10,1... | collective-permute-start | bytes 1216520 | tf_op jit(solution)/shard_map/ppermute | solution.py:450
  4.5 34.1 %collective-permute-start.1 = (f32[4,99,256]{2,1,0:T(8,128)S(1)}, f32[4,99,256]{2,1,0:T(8,128)S(1)}, u32[]{:S(2)}, u32[]{:S(2)}) collective-permute-start(f32[4,99,256]{2,1,0:T(8,128)S(1)} %pad_maximum_fusion.1), channel_id=1, source_target_pairs={{1,0},{2,1},{3,2},{4,3},{5,4},{6,5},{7,6},{8,7},{9,8},{10,9},{11,1... | collective-permute-start | bytes 1216520 | tf_op jit(solution)/shard_map/ppermute | solution.py:451
  38.6 0.8 %copy-start = (f32[4,99,256]{2,1,0:T(8,128)}, f32[4,99,256]{2,1,0:T(8,128)S(1)}, u32[]{:S(2)}) copy-start(f32[4,99,256]{2,1,0:T(8,128)S(1)} %collective-permute-done.refs_0_) | copy-start | bytes 1216516
  38.6 0.9 %copy-start.1 = (f32[4,99,256]{2,1,0:T(8,128)}, f32[4,99,256]{2,1,0:T(8,128)S(1)}, u32[]{:S(2)}) copy-start(f32[4,99,256]{2,1,0:T(8,128)S(1)} %collective-permute-done.1.refs_1_) | copy-start | bytes 1216516
where the time goes:
time: 46.1 us; the launch traced here: 45.6 us
  Pallas kernels  35.1 us (76%)
  starting transfers between devices  5.57 us (12%)
  local copies, waits for them, and re-layouts  4.76 us (10%)
    pallas_call x2, Pallas kernels, run_interior(): pl.pallas_call(functools.partial(interior, first, last, t0, t1, levels, l...  29 us
    pallas_call x1, Pallas kernels, run_edges(): pl.pallas_call(functools.partial(edges, levels, lon), out_shape=shape(lev...  6.08 us
    ppermute x1, starting transfers between devices, shards(): lax.ppermute(message(cotangent, coeffs, 0, 4), 'lon', [((i + 1) % count,...  5.06 us
    slice x3, local copies, waits for them, and re-layouts, message(): c[lo:hi]  2.16 us
    slice x1, local copies, waits for them, and re-layouts, message(): x[:, lo:hi, :].transpose(1, 0, 2)  1.51 us
    unnamed x6, local copies, waits for them, and re-layouts  1.05 us
  transfers between devices with their start and end apart: 2, of which 0 were waited for; matrix products, arithmetic and copies ran while one was open for 0% of the time, Pallas kernels for 64%

commit v1 on v0

--- a/solution.py
+++ b/solution.py
@@ -10,7 +10,8 @@
 
 G = 16
 H = 128
-VMEM_LIMIT = 56 * 1024 * 1024
+LIM_A, LIM_B = 28, 24
+EARLY, LATE = 4, 6
 COS1, COS2 = math.cos(2 * math.pi / 5), math.cos(4 * math.pi / 5)
 SIN1, SIN2 = math.sin(2 * math.pi / 5) ** 2, math.sin(4 * math.pi / 5) ** 2
 
@@ -28,8 +29,9 @@
     return high, low
 
 
-def prepare(depths_ref, syn_ref, ana_ref, cols_ref, ws_ref, wa_ref):
-    row = depths_ref[...]
+def prepare(small, at, cols_ref, ws_ref, wa_ref):
+    n = ws_ref.shape[0]
+    row = small[pl.ds(at + 2 * n, 1), :n]
     centre = 1.25 * row + 4.0
     half = 0.75 * row + 4.0
     product = row * (row + 4.0)
@@ -41,8 +43,7 @@
     cols_ref[2] = (1.0 - COS2) * (1.25 * d + 4.0)
     cols_ref[3] = SIN1 * (d * (d + 4.0))
     cols_ref[4] = SIN2 * (d * (d + 4.0))
-    n = row.shape[1]
-    for src, dst, scale in ((syn_ref[...].T, ws_ref, None), (ana_ref[...].T, wa_ref, gain)):
+    for src, dst, scale in ((small[at : at + n, :n].T, ws_ref, None), (small[at + n : at + 2 * n, :n].T, wa_ref, gain)):
         if scale is not None:
             src = src * scale
         high, low = split(src)
@@ -163,66 +164,66 @@
         flat[pl.ds(at + h * levels * 8, levels, stride=8), :] = value[:, h * H : (h + 1) * H]
 
 
-def interior(first, last, t0, t1, levels, lon, *refs):
+RESUME = (("r", (2, 3, 0)), ("u", (1, 2)), ("y", (0, 1)), ("w", (3, 0)), ("d1", (2,)), ("d2", (0, 1, 2)))
+CARRIED = sum(len(slots) for _, slots in RESUME)
+
+
+def interior(first, early, late, levels, lon, *refs):
     refs = list(refs)
     take = lambda n: [refs.pop(0) for _ in range(n)]
-    x_ref, metric_ref, east_ref, north_ref = take(4)
+    blocks = lon // 8
+    stop = jnp.where(lax.axis_index("lon") == 0, late, early)
+    half = lax.div(stop, 2)
     if first:
-        dep_ref, syn_ref, ana_ref = take(3)
+        x_ref, small = take(2)
+        save_ref, cols, ws, wa, co, to_west, to_east, carried, cbuf, obuf, zbuf = take(11)
+        (in_sem,) = take(1)
     else:
-        cols, ws, wa, r0, u0, y0, w0, e0, g0, _out_in = take(10)
-    out_ref, edge_ref, save_ref = take(3)
-    if first:
-        cols, ws, wa = take(3)
-    if not last:
-        state = take(6)
-    co, cbuf, obuf, zbuf, rr, uu, yy, ww, d1, d2, in_sem, out_sem = take(12)
+        cols, ws, wa, co, carried, cbuf, done, z_in = take(8)
+        out_ref, edge_ref, save_ref = take(3)
+        obuf, zbuf, out_sem = take(3)
+    rr, uu, yy, ww, d1, d2 = take(6)
     assert not refs
-
-    blocks = lon // 8
-    b_in0 = 0 if first else t0 // 2
-    b_in1 = blocks if last else t1 // 2 + 1
-    b_in1 = min(b_in1, blocks)
+    rings = {"r": rr, "u": uu, "y": yy, "w": ww, "d1": d1, "d2": d2}
 
     def fetch(b):
         return [
-            pltpu.make_async_copy(x_ref.at[:, pl.ds(8 * b, 8), pl.ds(h * H, H)], cbuf.at[b - b_in0, h], in_sem.at[h, b - b_in0])
+            pltpu.make_async_copy(x_ref.at[:, pl.ds(8 * b, 8), pl.ds(h * H, H)], cbuf.at[b, h], in_sem.at[h, b])
             for h in range(2)
         ]
 
-    b_out0 = 1 if first else (t0 - 1) // 2
-    b_out1 = blocks - 1 if last else (t1 - 1) // 2
-
-    def flush(b):
+    def flush(src, b):
         return [
-            pltpu.make_async_copy(
-                obuf.at[b - (b_out0 - 1), h], out_ref.at[:, pl.ds(8 * b, 8), pl.ds(h * H, H)], out_sem.at[h, b - b_out0])
+            pltpu.make_async_copy(src.at[b, h], out_ref.at[:, pl.ds(8 * b, 8), pl.ds(h * H, H)], out_sem.at[h, b])
             for h in range(2)
         ]
 
-    for b in range(b_in0, b_in1):
-        start(fetch(b))
-
-    co[0, pl.ds(0, 8), :] = jnp.zeros((8, 2 * H), jnp.float32)
-    fill_coefficients(co, 8, metric_ref[...], east_ref[...], north_ref[...])
     if first:
-        prepare(dep_ref, syn_ref, ana_ref, cols, ws, wa)
-    else:
-        for src, dst in ((r0, rr), (u0, uu), (y0, yy), (w0, ww), (e0, d1), (g0, d2)):
-            dst[...] = src[...]
+        for b in range(blocks):
+            start(fetch(b))
 
     rows_in = cbuf.reshape(cbuf.shape[0] * 2 * levels * 8, H)
     rows_out = obuf.reshape(obuf.shape[0] * 2 * levels * 8, H)
-
-    wait(fetch(b_in0))
     if first:
+        prepare(small, 3 * lon, cols, ws, wa)
+        co[0, pl.ds(0, 8), :] = jnp.zeros((8, 2 * H), jnp.float32)
+        fill_coefficients(co, 8, *(small[f * lon : (f + 1) * lon, :] for f in range(3)))
+        wait(fetch(0))
         rr[0] = mix(ws[...], load_row(rows_in, 0, 0, levels))
         save_ref[0, 0] = rr[0]
+    else:
+        lax.fori_loop(1, half - 1, lambda b, _: (start(flush(done, b)), 0)[1], 0)
+        n = 0
+        for name, slots in RESUME:
+            for slot in slots:
+                rings[name][slot] = carried[n]
+                n += 1
+        zbuf[...] = z_in[...]
+        obuf[half - 1] = done[half - 1]
 
     def finish(row):
         o = jnp.dot(wa[...], zbuf[...], preferred_element_type=jnp.float32)
-        b = lax.div(row + 8, 8) - 1 - (b_out0 - 1)
-        store_row(rows_out, b, lax.rem(row + 8, 8), levels, o)
+        store_row(rows_out, lax.div(row, 8), lax.rem(row, 8), levels, o)
 
     def store_z(rows, pair):
         start = rows.start
@@ -234,21 +235,18 @@
             zbuf[pl.ds(2 * levels + start, G), lanes] = high
 
     def body(t, _):
-        b = lax.div(t + 1, 2)
-
-        @pl.when((lax.rem(t, 2) == 1) & (b < b_in1) & (b > b_in0))
-        def _():
-            wait(fetch(b))
+        if first:
+            b = lax.div(t + 1, 2)
+
+            @pl.when((lax.rem(t, 2) == 1) & (b < blocks))
+            def _():
+                wait(fetch(b))
 
         for s in range(4):
             i = 4 * t + s
             nxt = i + 1
-            bb = lax.div(nxt, 8) - b_in0
-            finish_row = i - 5
-            if first:
-                finish_row = jnp.maximum(finish_row, 0)
-            finish(finish_row)
-            rr[(s + 1) % 4] = mix(ws[...], load_row(rows_in, bb, lax.rem(nxt, 8), levels))
+            finish(jnp.maximum(i - 5, 0) if first else i - 5)
+            rr[(s + 1) % 4] = mix(ws[...], load_row(rows_in, lax.div(nxt, 8), lax.rem(nxt, 8), levels))
             k = 8 + i
             q = lambda n: (s + n) % 4
             step1(levels, cols, co, k - 1, (rr, q(3)), (rr, q(0)), (rr, q(2)), (uu, q(3)), (d1, q(3)), (d2, q(3)))
@@ -272,43 +270,55 @@
                 save_ref[3, 0] = ww[3]
                 save_ref[3, 1] = ww[0]
 
-        bo = lax.div(t - 3, 2)
-
-        @pl.when((lax.rem(t, 2) == 1) & (t >= 3) & (bo >= b_out0) & (bo < b_out1))
-        def _():
-            start(flush(bo))
+        if not first:
+            bo = lax.div(t - 3, 2)
+
+            @pl.when((lax.rem(t, 2) == 1) & (bo >= 1) & (bo < blocks - 2))
+            def _():
+                start(flush(obuf, bo))
 
         return 0
 
-    lax.fori_loop(t0, t1, body, 0)
-    finish(jnp.int32(4 * t1 - 5))
-    if not last:
-        start(flush(b_out1 - 1))
-        for src, dst in zip((rr, uu, yy, ww, d1, d2), state):
-            dst[...] = src[...]
     if first:
-        edge_ref[...] = obuf[0]
+        lax.fori_loop(0, stop, body, 0)
+        n = 0
+        for name, slots in RESUME:
+            for slot in slots:
+                carried[n] = rings[name][slot]
+                n += 1
+        lax.fori_loop(half + 1, blocks, lambda b, _: (wait(fetch(b)), 0)[1], 0)
+        for j in range(8):
+            msg_ref = (to_west, to_east)[j // 4]
+            block, row = ((0, j), (blocks - 1, j))[j // 4]
+            at = j if j < 4 else lon - 8 + j
+            msg_ref[j % 4, :levels, :] = load_row(rows_in, block, row, levels)
+            for f in range(3):
+                msg_ref[j % 4, pl.ds(levels + f, 1), :] = small[pl.ds(f * lon + at, 1), :]
     else:
-        edge_ref[...] = obuf[blocks - 1 - (b_out0 - 1)]
-    if last:
-        at = 4 * t1
-        for f, (ref, row) in enumerate(((rr, at - 2), (uu, at - 3), (yy, at - 4), (ww, at - 5))):
+        lax.fori_loop(stop, lon // 4, body, 0)
+        finish(lon - 5)
+        edge_ref[0] = obuf[blocks - 2]
+        edge_ref[1] = obuf[blocks - 1]
+        for f, (ref, row) in enumerate(((rr, lon - 2), (uu, lon - 3), (yy, lon - 4), (ww, lon - 5))):
             save_ref[f, 0] = ref[row % 4]
             save_ref[f, 1] = ref[(row + 1) % 4]
-    for b in range(b_out0, b_out1):
-        wait(flush(b))
+        lax.fori_loop(1, blocks - 2, lambda b, _: (wait(flush(obuf, b)), 0)[1], 0)
 
 
 def edges(levels, lon, *refs):
-    (hl, hr, metric_ref, east_ref, north_ref, cols, ws, wa, save_l, save_r, edge_l, edge_r, _out_in,
+    (hl, hr, small, cols, ws, wa, save_l, save_r, edge_l, edge_r, _out_in,
      out_ref, co, rr, uu, yy, ww, d1, d2, zbuf, obuf, sems) = refs
-    copies = []
+    copies = [
+        pltpu.make_async_copy(edge_r.at[0, h], out_ref.at[:, pl.ds(lon - 16, 8), pl.ds(h * H, H)], sems.at[2, h])
+        for h in range(2)
+    ]
+    start(copies)
     for side in range(2):
         halo = hr if side else hl
         c = co.at[side]
         c[0, pl.ds(0, 8), :] = jnp.zeros((8, 2 * H), jnp.float32)
-        own = pl.ds(lon - 8, 8) if side else pl.ds(0, 8)
-        mine = (metric_ref[own, :], east_ref[own, :], north_ref[own, :])
+        own = lon - 8 if side else 0
+        mine = tuple(small[pl.ds(f * lon + own, 8), :] for f in range(3))
         theirs = [halo[:, levels + f, :] for f in range(3)]
         if side:
             window = [jnp.concatenate([a, b], axis=0) for a, b in zip(mine, theirs)]
@@ -320,7 +330,7 @@
         r, u, y, w = rr.at[side], uu.at[side], yy.at[side], ww.at[side]
         e, g = d1.at[side], d2.at[side]
         save = save_r if side else save_l
-        edge = edge_r if side else edge_l
+        edge = edge_r.at[1] if side else edge_l.at[0]
         new_r = 4 if side else 0
         for j in range(4):
             r[new_r + j] = mix(ws[...], halo[j, :levels, :])
@@ -372,6 +382,7 @@
 
 
 F32, BF16 = jnp.float32, jnp.bfloat16
+HBM = pl.BlockSpec(memory_space=pltpu.HBM)
 ANY = pl.BlockSpec(memory_space=pl.ANY)
 VM = pl.BlockSpec(memory_space=pltpu.VMEM)
 
@@ -380,80 +391,76 @@
     return jax.ShapeDtypeStruct(dims, dtype)
 
 
-def run_interior(first, last, t0, t1, levels, lon, lat, args, state, out_prev):
-    ring = lambda: pltpu.VMEM((4, levels, lat), F32)
-    outs = [(shape(levels, lon, lat), ANY), (shape(2, levels, 8, H), VM), (shape(4, 2, levels, lat), VM)]
+def params(mib):
+    return pltpu.CompilerParams(vmem_limit_bytes=mib * 1024 * 1024)
+
+
+def run_interior(first, levels, lon, lat, operands):
+    ring = pltpu.VMEM((4, levels, lat), F32)
+    blocks = lon // 8
+    mixer = shape(levels, 3 * levels, dtype=BF16)
+    saved = shape(4, 2, levels, lat)
     if first:
-        outs += [(shape(5, levels, H), VM), (shape(levels, 3 * levels, dtype=BF16), VM), (shape(levels, 3 * levels, dtype=BF16), VM)]
-    if not last:
-        outs += [(shape(4, levels, lat), VM)] * 6
-    blocks = lon // 8
-    operands = list(args) + list(state)
-    specs = [ANY] + [VM] * (len(operands) - 1)
-    aliases = {}
-    if out_prev is not None:
-        aliases[len(operands)] = 0
-        operands.append(out_prev)
-        specs.append(ANY)
+        outs = [saved, shape(5, levels, H), mixer, mixer, shape(5, lon + 8, lat), shape(4, levels + 8, lat), shape(4, levels + 8, lat),
+                shape(CARRIED, levels, lat), shape(blocks + 1, 2, levels, 8, H), shape(LATE // 2, 2, levels, 8, H),
+                shape(3 * levels, lat, dtype=BF16)]
+        in_specs = [HBM, VM]
+        out_specs = [VM] * len(outs)
+        scratch = [pltpu.SemaphoreType.DMA((2, blocks))]
+    else:
+        outs = [shape(levels, lon, lat), shape(2, 2, levels, 8, H), saved]
+        in_specs = [VM] * 8
+        out_specs = [HBM, VM, VM]
+        scratch = [pltpu.VMEM((blocks, 2, levels, 8, H), F32), pltpu.VMEM((3 * levels, lat), BF16),
+                   pltpu.SemaphoreType.DMA((2, blocks))]
     return pl.pallas_call(
-        functools.partial(interior, first, last, t0, t1, levels, lon),
-        out_shape=[o for o, _ in outs],
-        in_specs=specs,
-        out_specs=[s for _, s in outs],
-        input_output_aliases=aliases,
-        scratch_shapes=[
-            pltpu.VMEM((5, lon + 8, lat), F32),
-            pltpu.VMEM((blocks + 1, 2, levels, 8, H), F32),
-            pltpu.VMEM((blocks + 1, 2, levels, 8, H), F32),
-            pltpu.VMEM((3 * levels, lat), BF16),
-            ring(), ring(), ring(), ring(), ring(), ring(),
-            pltpu.SemaphoreType.DMA((2, blocks + 1)),
-            pltpu.SemaphoreType.DMA((2, blocks + 1)),
-        ],
-        compiler_params=pltpu.CompilerParams(vmem_limit_bytes=VMEM_LIMIT),
+        functools.partial(interior, first, EARLY, LATE, levels, lon),
+        out_shape=outs,
+        in_specs=in_specs,
+        out_specs=out_specs,
+        scratch_shapes=scratch + [ring, ring, ring, ring, ring, ring],
+        compiler_params=params(LIM_A if first else LIM_B),
         name="interior",
     )(*operands)
 
 
 def run_edges(levels, lon, lat, operands):
+    window = lambda n: pltpu.VMEM((2, n, levels, lat), F32)
     return pl.pallas_call(
         functools.partial(edges, levels, lon),
         out_shape=shape(levels, lon, lat),
-        in_specs=[VM] * 12 + [ANY],
-        out_specs=ANY,
-        input_output_aliases={12: 0},
+        in_specs=[VM] * 10 + [HBM],
+        out_specs=HBM,
+        input_output_aliases={10: 0},
         scratch_shapes=[
             pltpu.VMEM((2, 5, 24, lat), F32),
-            pltpu.VMEM((2, 8, levels, lat), F32),
-            pltpu.VMEM((2, 8, levels, lat), F32),
-            pltpu.VMEM((2, 8, levels, lat), F32),
-            pltpu.VMEM((2, 10, levels, lat), F32),
-            pltpu.VMEM((2, 8, levels, lat), F32),
-            pltpu.VMEM((2, 8, levels, lat), F32),
+            window(8), window(8), window(8), window(10), window(8), window(8),
             pltpu.VMEM((2, 4, 3 * levels, lat), BF16),
             pltpu.VMEM((2, 2, levels, 8, H), F32),
-            pltpu.SemaphoreType.DMA((2, 2)),
+            pltpu.SemaphoreType.DMA((3, 2)),
         ],
-        compiler_params=pltpu.CompilerParams(vmem_limit_bytes=VMEM_LIMIT),
+        compiler_params=params(LIM_B),
         name="edges",
     )(*operands)
 
 
-def message(x, coeffs, lo, hi):
-    return jnp.concatenate([x[:, lo:hi, :].transpose(1, 0, 2), jnp.stack([c[lo:hi] for c in coeffs], axis=1)], axis=1)
-
-
 def shards(cotangent, synthesis, analysis, depths, metric, east_face, north_face):
     levels, lon, lat = cotangent.shape
-    coeffs = (metric, east_face, north_face)
     count = lax.axis_size("lon")
-    from_west = lax.ppermute(message(cotangent, coeffs, lon - 4, lon), "lon", [(i, (i + 1) % count) for i in range(count)])
-    from_east = lax.ppermute(message(cotangent, coeffs, 0, 4), "lon", [((i + 1) % count, i) for i in range(count)])
-    args = (cotangent,) + coeffs
-    out, edge_l, save_l, cols, ws, wa, *state = run_interior(
-        True, False, 0, 7, levels, lon, lat, args + (depths.reshape(1, -1), synthesis, analysis), (), None)
-    out, edge_r, save_r = run_interior(False, True, 7, lon // 4, levels, lon, lat, args, (cols, ws, wa, *state), out)
-    return run_edges(levels, lon, lat, (from_west, from_east) + coeffs + (cols, ws, wa, save_l, save_r, edge_l, edge_r, out))
+    parts = [metric, east_face, north_face, synthesis, analysis, depths[None]]
+    total = 3 * lon + 2 * levels + 8
+    small, at = 0.0, 0
+    for part in parts:
+        rows, width = part.shape
+        small = small + jnp.pad(part, ((at, total - at - rows), (0, lat - width)))
+        at += rows
+    save_l, cols, ws, wa, co, to_west, to_east, carried, blocks_in, blocks_out, z = run_interior(
+        True, levels, lon, lat, (cotangent, small))
+    from_west = lax.ppermute(to_east, "lon", [(i, (i + 1) % count) for i in range(count)])
+    from_east = lax.ppermute(to_west, "lon", [((i + 1) % count, i) for i in range(count)])
+    out, edge_r, save_r = run_interior(
+        False, levels, lon, lat, (cols, ws, wa, co, carried, blocks_in, blocks_out, z))
+    return run_edges(levels, lon, lat, (from_west, from_east, small, cols, ws, wa, save_l, save_r, blocks_out, edge_r, out))
 
 
 def solution(mesh):

time: 46.1 us -> 33.4 us (0.72)
  Pallas kernels: 35.1 us -> 24.8 us
  local copies, waits for them, and re-layouts: 4.76 us -> 2.78 us
  starting transfers between devices: 5.57 us -> 4.49 us
  other arithmetic: 0.07 us -> 1 us
    pallas_call x2, Pallas kernels: 29 us -> 20.7 us  [run_interior(): pl.pallas_call(functools.partial(interior, first, EARLY, LATE, levels, lo...]
    slice x4 -> x0, local copies, waits for them, and re-layouts: 3.67 us -> none  [the longest x3 2.16 us: message(): c[lo:hi]]
    pallas_call x1, Pallas kernels: 6.08 us -> 4.15 us  [run_edges(): pl.pallas_call(functools.partial(edges, levels, lon), out_shape=shape(lev...]
    unnamed x6 -> x2, local copies, waits for them, and re-layouts: 1.05 us -> 2.78 us
    ppermute x2, starting transfers between devices: 5.57 us -> 4.49 us  [the longest x1 4.43 us: shards(): lax.ppermute(to_west, 'lon', [((i + 1) % count, i) for i in range(count)])]
    add x0 -> x1, other arithmetic: none -> 1 us  [shards(): small = small + jnp.pad(part, ((at, total - at - rows), (0, lat - width)))]
  transfers between devices with their start and end apart: 2 -> 2, of which waited for: 0 -> 0; matrix products, arithmetic and copies ran while one was open for 0% -> 0% of each run, Pallas kernels for 64% -> 36%
where the time goes in v1:
time: 33.4 us; the launch traced here: 33.2 us
  Pallas kernels  24.8 us (74%)
  starting transfers between devices  4.49 us (13%)
  local copies, waits for them, and re-layouts  2.78 us (8%)
  other arithmetic  1 us (3%)
    pallas_call x2, Pallas kernels, run_interior(): pl.pallas_call(functools.partial(interior, first, EARLY, LATE, levels, lo...  20.7 us
    ppermute x1, starting transfers between devices, shards(): lax.ppermute(to_west, 'lon', [((i + 1) % count, i) for i in range(count)])  4.43 us
    pallas_call x1, Pallas kernels, run_edges(): pl.pallas_call(functools.partial(edges, levels, lon), out_shape=shape(lev...  4.15 us
    unnamed x2, local copies, waits for them, and re-layouts  2.78 us
    add x1, other arithmetic, shards(): small = small + jnp.pad(part, ((at, total - at - rows), (0, lat - width)))  1 us
  transfers between devices with their start and end apart: 2, of which 0 were waited for; matrix products, arithmetic and copies ran while one was open for 0% of the time, Pallas kernels for 36%

profile of v1, /device:TPU:0, one launch (start us, length us, event | category | flops | bytes accessed | tf_op | source)
XLA Modules:
  0.0 33.2 jit_solution(17111353303431197305)
XLA Ops:
  0.0 1.0 %pad_add_fusion.refs_1_.refs_2_ = f32[392,256]{1,0:T(8,128)S(1)} fusion(f32[1,96]{1,0:T(1,128)} %bitcast.1, f32[96,96]{1,0:T(8,128)} %param.9, f32[96,96]{1,0:T(8,128)} %param.8, f32[64,256]{1,0:T(8,128)} %param.13, f32[64,256]{1,0:T(8,128)} %param.12, f32[64,256]{1,0:T(8,128)} %param.11), kind=kLoop, calls=%fused_computation | loop fusion | flops 501760 | bytes 672128 | tf_op jit(solution)/shard_map/add | solution.py:455
  1.0 0.0 copy-start
  1.0 2.8 %copy-done = f32[96,64,256]{2,1,0:T(8,128)S(1)} copy-done((f32[96,64,256]{2,1,0:T(8,128)S(1)}, f32[96,64,256]{2,1,0:T(8,128)}, u32[]{:S(2)}) %copy-start) | copy-done | bytes 6291480
  3.8 8.7 %interior.2 = (f32[4,2,96,256]{3,2,1,0:T(8,128)S(1)}, f32[5,96,128]{2,1,0:T(8,128)S(1)}, bf16[96,288]{1,0:T(8,128)(2,1)S(1)}, bf16[96,288]{1,0:T(8,128)(2,1)S(1)...) custom-call(f32[96,64,256]{2,1,0:T(8,128)S(1)} %copy-done, ...), custom_call_target="tpu_custom_call" | custom-call | tf_op jit(solution)/shard_map/interior/pallas_call | solution.py:416
  12.5 0.1 collective-permute-start
  12.5 4.4 %collective-permute-start.1 = (f32[4,104,256]{2,1,0:T(8,128)S(1)}, f32[4,104,256]{2,1,0:T(8,128)S(1)}, u32[]{:S(2)}, u32[]{:S(2)}) collective-permute-start(f32[4,104,256]{2,1,0:T(8,128)S(1)} %get-tuple-element.20), channel_id=1, source_target_pairs={{1,0},{2,1},{3,2},{4,3},{5,4},{6,5},{7,6},{8,7},{9,8},{10,9},{11,1... | collective-permute-start | bytes 1277960 | tf_op jit(solution)/shard_map/ppermute | solution.py:460
  17.0 12.0 %interior.3 = (f32[96,64,256]{2,1,0:T(8,128)}, f32[2,2,96,8,128]{4,3,2,1,0:T(8,128)S(1)}, f32[4,2,96,256]{3,2,1,0:T(8,128)S(1)}) custom-call(f32[5,96,128]{2,1,0:T(8,128)S(1)} %get-tuple-element.21.refs_0_.refs_3_, bf16[96,288]{1,0:T(8,128)(2,1)S(1)} %get-tuple-element.22.refs_1_.refs_4_, bf16[96,288]{1,0:T(8,128)(2,1)S(1)} %get-tuple-element.23.refs_2_.refs_5_, ...), custom_call_target="tpu_custom_call" | custom-call | tf_op jit(solution)/shard_map/interior/pallas_call | solution.py:416
  29.0 0.0 collective-permute-done.refs_0_
  29.0 0.0 collective-permute-done.1.refs_1_
  29.0 4.1 %edges.1 = f32[96,64,256]{2,1,0:T(8,128)} custom-call(f32[4,104,256]{2,1,0:T(8,128)S(1)} %collective-permute-done.refs_0_, f32[4,104,256]{2,1,0:T(8,128)S(1)} %collective-permute-done.1.refs_1_, f32[392,256]{1,0:T(8,128)S(1)} %pad_add_fusion.refs_1_.refs_2_, f32[5,96,128]{2,1,0:T(8,128)S(1)} %get-tuple-element.21.refs_0_.refs_3_, ...), custom_call_target="tpu_custom_call", output_to_operand_aliasing={{}: (10, {})} | custom-call | tf_op jit(solution)/shard_map/edges/pallas_call | solution.py:429
Async XLA Ops:
  1.0 2.8 %copy-start = (f32[96,64,256]{2,1,0:T(8,128)S(1)}, f32[96,64,256]{2,1,0:T(8,128)}, u32[]{:S(2)}) copy-start(f32[96,64,256]{2,1,0:T(8,128)} %refs_0_.1) | copy-start | bytes 18874372
  12.5 16.5 %collective-permute-start = (f32[4,104,256]{2,1,0:T(8,128)S(1)}, f32[4,104,256]{2,1,0:T(8,128)S(1)}, u32[]{:S(2)}, u32[]{:S(2)}) collective-permute-start(f32[4,104,256]{2,1,0:T(8,128)S(1)} %get-tuple-element.19), channel_id=1, source_target_pairs={{0,1},{1,2},{2,3},{3,4},{4,5},{5,6},{6,7},{7,8},{8,9},{9,10},{10,1... | collective-permute-start | bytes 1277960 | tf_op jit(solution)/shard_map/ppermute | solution.py:459
  12.5 16.5 %collective-permute-start.1 = (f32[4,104,256]{2,1,0:T(8,128)S(1)}, f32[4,104,256]{2,1,0:T(8,128)S(1)}, u32[]{:S(2)}, u32[]{:S(2)}) collective-permute-start(f32[4,104,256]{2,1,0:T(8,128)S(1)} %get-tuple-element.20), channel_id=1, source_target_pairs={{1,0},{2,1},{3,2},{4,3},{5,4},{6,5},{7,6},{8,7},{9,8},{10,9},{11,1... | collective-permute-start | bytes 1277960 | tf_op jit(solution)/shard_map/ppermute | solution.py:460

commit v2 on v1

--- a/solution.py
+++ b/solution.py
@@ -11,7 +11,7 @@
 G = 16
 H = 128
 LIM_A, LIM_B = 28, 24
-EARLY, LATE = 4, 6
+EARLY, LATE = 2, 3
 COS1, COS2 = math.cos(2 * math.pi / 5), math.cos(4 * math.pi / 5)
 SIN1, SIN2 = math.sin(2 * math.pi / 5) ** 2, math.sin(4 * math.pi / 5) ** 2
 
@@ -29,7 +29,10 @@
     return high, low
 
 
-def prepare(small, at, cols_ref, ws_ref, wa_ref):
+def prepare(lon, small, cols_ref, ws_ref, wa_ref, co):
+    at = 3 * lon
+    co[0, pl.ds(0, 8), :] = jnp.zeros((8, 2 * H), jnp.float32)
+    fill_coefficients(co, 8, *(small[f * lon : (f + 1) * lon, :] for f in range(3)))
     n = ws_ref.shape[0]
     row = small[pl.ds(at + 2 * n, 1), :n]
     centre = 1.25 * row + 4.0
@@ -115,6 +118,10 @@
     return (ta - a1, tb - a1), (ta - a2, tb - a2)
 
 
+def add_scaled(pair, scale, old):
+    return pair[0] + scale * old[0], pair[1] + scale * old[1]
+
+
 def groups(levels):
     return [pl.ds(g * G, G) for g in range(levels // G)]
 
@@ -172,11 +179,10 @@
     refs = list(refs)
     take = lambda n: [refs.pop(0) for _ in range(n)]
     blocks = lon // 8
-    stop = jnp.where(lax.axis_index("lon") == 0, late, early)
-    half = lax.div(stop, 2)
+    stop = jnp.where(lax.axis_index("lon") < 2, late, early)
     if first:
-        x_ref, small = take(2)
-        save_ref, cols, ws, wa, co, to_west, to_east, carried, cbuf, obuf, zbuf = take(11)
+        x_ref, small, cols, ws, wa, co = take(6)
+        save_ref, near, far, carried, cbuf, obuf, zbuf = take(7)
         (in_sem,) = take(1)
     else:
         cols, ws, wa, co, carried, cbuf, done, z_in = take(8)
@@ -205,21 +211,18 @@
     rows_in = cbuf.reshape(cbuf.shape[0] * 2 * levels * 8, H)
     rows_out = obuf.reshape(obuf.shape[0] * 2 * levels * 8, H)
     if first:
-        prepare(small, 3 * lon, cols, ws, wa)
-        co[0, pl.ds(0, 8), :] = jnp.zeros((8, 2 * H), jnp.float32)
-        fill_coefficients(co, 8, *(small[f * lon : (f + 1) * lon, :] for f in range(3)))
         wait(fetch(0))
         rr[0] = mix(ws[...], load_row(rows_in, 0, 0, levels))
         save_ref[0, 0] = rr[0]
     else:
-        lax.fori_loop(1, half - 1, lambda b, _: (start(flush(done, b)), 0)[1], 0)
+        lax.fori_loop(1, stop - 1, lambda b, _: (start(flush(done, b)), 0)[1], 0)
         n = 0
         for name, slots in RESUME:
             for slot in slots:
                 rings[name][slot] = carried[n]
                 n += 1
         zbuf[...] = z_in[...]
-        obuf[half - 1] = done[half - 1]
+        obuf[stop - 1] = done[stop - 1]
 
     def finish(row):
         o = jnp.dot(wa[...], zbuf[...], preferred_element_type=jnp.float32)
@@ -234,68 +237,84 @@
             zbuf[pl.ds(levels + start, G), lanes] = low
             zbuf[pl.ds(2 * levels + start, G), lanes] = high
 
+    def advance(t, s, stages):
+        i = 8 * t + s
+        k = 8 + i
+        q = lambda n: (s + n) % 4
+        if stages == 4:
+            finish(i - 5)
+        rr[(s + 1) % 4] = mix(ws[...], load_row(rows_in, t + (s + 1) // 8, (s + 1) % 8, levels))
+        if not stages:
+            return
+        for rows in groups(levels):
+            c1, c2, c3, c4 = (coefficients(co, k - min(n, stages)) for n in range(1, 5))
+            at = lambda ref, n: halves(ref, q(n), rows)
+            first_diag, second_diag = diagonals(cols, co, k - 1, rows)
+            put(d1, q(3), rows, first_diag)
+            put(d2, q(3), rows, second_diag)
+            r = at(rr, 2)
+            u = operate(first_diag, at(rr, 3), at(rr, 0), r, c1)
+            put(uu, q(3), rows, u)
+            if stages < 2:
+                continue
+            y = add_scaled(operate(at(d1, 2), at(uu, 2), u, at(uu, 1), c2), cols[3, rows, :], r)
+            put(yy, q(2), rows, y)
+            if stages < 3:
+                continue
+            old = at(yy, 0)
+            w = operate(at(d2, 1), at(yy, 1), y, old, c3)
+            put(ww, q(1), rows, w)
+            if stages < 4:
+                continue
+            store_z(rows, add_scaled(operate(at(d2, 0), at(ww, 0), w, at(ww, 3), c4), cols[4, rows, :], old))
+
     def body(t, _):
         if first:
-            b = lax.div(t + 1, 2)
-
-            @pl.when((lax.rem(t, 2) == 1) & (b < blocks))
+
+            @pl.when(t + 1 < blocks)
             def _():
-                wait(fetch(b))
-
-        for s in range(4):
-            i = 4 * t + s
-            nxt = i + 1
-            finish(jnp.maximum(i - 5, 0) if first else i - 5)
-            rr[(s + 1) % 4] = mix(ws[...], load_row(rows_in, lax.div(nxt, 8), lax.rem(nxt, 8), levels))
-            k = 8 + i
-            q = lambda n: (s + n) % 4
-            step1(levels, cols, co, k - 1, (rr, q(3)), (rr, q(0)), (rr, q(2)), (uu, q(3)), (d1, q(3)), (d2, q(3)))
-            step_even(levels, cols, 3, co, k - 2, (uu, q(2)), (uu, q(3)), (uu, q(1)), (rr, q(2)), (d1, q(2)),
-                      lambda rows, pair, at=q(2): put(yy, at, rows, pair))
-            step3(levels, co, k - 3, (yy, q(1)), (yy, q(2)), (yy, q(0)), (d2, q(1)), (ww, q(1)))
-            step_even(levels, cols, 4, co, k - 4, (ww, q(0)), (ww, q(1)), (ww, q(3)), (yy, q(0)), (d2, q(0)), store_z)
-
-        if first:
-
-            @pl.when(t == 0)
+                wait(fetch(t + 1))
+
+        for s in range(8):
+            advance(t, s, 4)
+
+        if not first:
+
+            @pl.when(t < blocks - 1)
             def _():
+                start(flush(obuf, t - 1))
+
+        return 0
+
+    if first:
+        wait(fetch(1))
+        for s in range(8):
+            advance(0, s, s // 2)
+            if s == 3:
                 save_ref[0, 1] = rr[1]
                 save_ref[1, 0] = uu[1]
                 save_ref[1, 1] = uu[2]
-
-            @pl.when(t == 1)
-            def _():
-                save_ref[2, 0] = yy[2]
-                save_ref[2, 1] = yy[3]
-                save_ref[3, 0] = ww[3]
-                save_ref[3, 1] = ww[0]
-
-        if not first:
-            bo = lax.div(t - 3, 2)
-
-            @pl.when((lax.rem(t, 2) == 1) & (bo >= 1) & (bo < blocks - 2))
-            def _():
-                start(flush(obuf, bo))
-
-        return 0
-
-    if first:
-        lax.fori_loop(0, stop, body, 0)
+        save_ref[2, 0] = yy[2]
+        save_ref[2, 1] = yy[3]
+        save_ref[3, 0] = ww[3]
+        save_ref[3, 1] = ww[0]
+        lax.fori_loop(1, stop, body, 0)
         n = 0
         for name, slots in RESUME:
             for slot in slots:
                 carried[n] = rings[name][slot]
                 n += 1
-        lax.fori_loop(half + 1, blocks, lambda b, _: (wait(fetch(b)), 0)[1], 0)
-        for j in range(8):
-            msg_ref = (to_west, to_east)[j // 4]
-            block, row = ((0, j), (blocks - 1, j))[j // 4]
-            at = j if j < 4 else lon - 8 + j
-            msg_ref[j % 4, :levels, :] = load_row(rows_in, block, row, levels)
-            for f in range(3):
-                msg_ref[j % 4, pl.ds(levels + f, 1), :] = small[pl.ds(f * lon + at, 1), :]
+        lax.fori_loop(stop + 1, blocks, lambda b, _: (wait(fetch(b)), 0)[1], 0)
+        even = lax.rem(lax.axis_index("lon"), 2) == 0
+        for msg_ref, east in ((near, even), (far, jnp.logical_not(even))):
+            block, row = jnp.where(east, blocks - 1, 0), jnp.where(east, 4, 0)
+            at = jnp.where(east, lon - 4, 0)
+            for j in range(4):
+                msg_ref[j, :levels, :] = load_row(rows_in, block, row + j, levels)
+                for f in range(3):
+                    msg_ref[j, pl.ds(levels + f, 1), :] = small[pl.ds(f * lon + at + j, 1), :]
     else:
-        lax.fori_loop(stop, lon // 4, body, 0)
+        lax.fori_loop(stop, blocks, body, 0)
         finish(lon - 5)
         edge_ref[0] = obuf[blocks - 2]
         edge_ref[1] = obuf[blocks - 1]
@@ -306,15 +325,18 @@
 
 
 def edges(levels, lon, *refs):
-    (hl, hr, small, cols, ws, wa, save_l, save_r, edge_l, edge_r, _out_in,
-     out_ref, co, rr, uu, yy, ww, d1, d2, zbuf, obuf, sems) = refs
+    (near, far, small, cols, ws, wa, save_l, save_r, edge_l, edge_r, _out_in,
+     out_ref, co, rr, uu, yy, ww, d1, d2, zbuf, obuf, halos, sems) = refs
+    odd = lax.rem(lax.axis_index("lon"), 2)
+    halos[1 - odd] = near[...]
+    halos[odd] = far[...]
     copies = [
         pltpu.make_async_copy(edge_r.at[0, h], out_ref.at[:, pl.ds(lon - 16, 8), pl.ds(h * H, H)], sems.at[2, h])
         for h in range(2)
     ]
     start(copies)
     for side in range(2):
-        halo = hr if side else hl
+        halo = halos.at[side]
         c = co.at[side]
         c[0, pl.ds(0, 8), :] = jnp.zeros((8, 2 * H), jnp.float32)
         own = lon - 8 if side else 0
@@ -395,16 +417,28 @@
     return pltpu.CompilerParams(vmem_limit_bytes=mib * 1024 * 1024)
 
 
+def run_prepare(levels, lon, lat, small):
+    mixer = shape(levels, 3 * levels, dtype=BF16)
+    return pl.pallas_call(
+        functools.partial(prepare, lon),
+        out_shape=[shape(5, levels, H), mixer, mixer, shape(5, lon + 8, lat)],
+        in_specs=[VM],
+        out_specs=[VM] * 4,
+        compiler_params=params(16),
+        cost_estimate=pl.CostEstimate(flops=2 * 10**9, bytes_accessed=2**20, transcendentals=0),
+        name="prepare",
+    )(small)
+
+
 def run_interior(first, levels, lon, lat, operands):
     ring = pltpu.VMEM((4, levels, lat), F32)
     blocks = lon // 8
-    mixer = shape(levels, 3 * levels, dtype=BF16)
     saved = shape(4, 2, levels, lat)
     if first:
-        outs = [saved, shape(5, levels, H), mixer, mixer, shape(5, lon + 8, lat), shape(4, levels + 8, lat), shape(4, levels + 8, lat),
-                shape(CARRIED, levels, lat), shape(blocks + 1, 2, levels, 8, H), shape(LATE // 2, 2, levels, 8, H),
+        outs = [saved, shape(4, levels + 8, lat), shape(4, levels + 8, lat),
+                shape(CARRIED, levels, lat), shape(blocks + 1, 2, levels, 8, H), shape(LATE, 2, levels, 8, H),
                 shape(3 * levels, lat, dtype=BF16)]
-        in_specs = [HBM, VM]
+        in_specs = [HBM] + [VM] * 5
         out_specs = [VM] * len(outs)
         scratch = [pltpu.SemaphoreType.DMA((2, blocks))]
     else:
@@ -437,6 +471,7 @@
             window(8), window(8), window(8), window(10), window(8), window(8),
             pltpu.VMEM((2, 4, 3 * levels, lat), BF16),
             pltpu.VMEM((2, 2, levels, 8, H), F32),
+            pltpu.VMEM((2, 4, levels + 8, lat), F32),
             pltpu.SemaphoreType.DMA((3, 2)),
         ],
         compiler_params=params(LIM_B),
@@ -454,13 +489,14 @@
         rows, width = part.shape
         small = small + jnp.pad(part, ((at, total - at - rows), (0, lat - width)))
         at += rows
-    save_l, cols, ws, wa, co, to_west, to_east, carried, blocks_in, blocks_out, z = run_interior(
-        True, levels, lon, lat, (cotangent, small))
-    from_west = lax.ppermute(to_east, "lon", [(i, (i + 1) % count) for i in range(count)])
-    from_east = lax.ppermute(to_west, "lon", [((i + 1) % count, i) for i in range(count)])
+    cols, ws, wa, co = run_prepare(levels, lon, lat, small)
+    save_l, near, far, carried, blocks_in, blocks_out, z = run_interior(
+        True, levels, lon, lat, (cotangent, small, cols, ws, wa, co))
+    near = lax.ppermute(near, "lon", [(i, i ^ 1) for i in range(count)])
+    far = lax.ppermute(far, "lon", [(i, (i + 2 * (i % 2) - 1) % count) for i in range(count)])
     out, edge_r, save_r = run_interior(
         False, levels, lon, lat, (cols, ws, wa, co, carried, blocks_in, blocks_out, z))
-    return run_edges(levels, lon, lat, (from_west, from_east, small, cols, ws, wa, save_l, save_r, blocks_out, edge_r, out))
+    return run_edges(levels, lon, lat, (near, far, small, cols, ws, wa, save_l, save_r, blocks_out, edge_r, out))
 
 
 def solution(mesh):

time: 33.4 us -> 29.8 us (0.89)
  Pallas kernels: 24.8 us -> 22.9 us
  local copies, waits for them, and re-layouts: 2.78 us -> 1.57 us
  starting transfers between devices: 4.49 us -> 4.04 us
    pallas_call x2, Pallas kernels: 20.7 us -> 18.5 us  [run_interior(): pl.pallas_call(functools.partial(interior, first, EARLY, LATE, levels, lo...]
    unnamed x2, local copies, waits for them, and re-layouts: 2.78 us -> 1.57 us
    ppermute x2, starting transfers between devices: 4.49 us -> 4.04 us  [the longest x1 3.53 us: shards(): lax.ppermute(far, 'lon', [(i, (i + 2 * (i % 2) - 1) % count) for i in ran...]
  transfers between devices with their start and end apart: 2 -> 2, of which waited for: 0 -> 0; matrix products, arithmetic and copies ran while one was open for 0% -> 0% of each run, Pallas kernels for 36% -> 39%
where the time goes in v2:
time: 29.8 us; the launch traced here: 29.7 us
  Pallas kernels  22.9 us (77%)
  starting transfers between devices  4.04 us (14%)
  local copies, waits for them, and re-layouts  1.57 us (5%)
  other arithmetic  1.14 us (4%)
    pallas_call x2, Pallas kernels, run_interior(): pl.pallas_call(functools.partial(interior, first, EARLY, LATE, levels, lo...  18.5 us
    pallas_call x1, Pallas kernels, run_edges(): pl.pallas_call(functools.partial(edges, levels, lon), out_shape=shape(lev...  4.16 us
    ppermute x1, starting transfers between devices, shards(): lax.ppermute(far, 'lon', [(i, (i + 2 * (i % 2) - 1) % count) for i in ran...  3.53 us
    unnamed x2, local copies, waits for them, and re-layouts  1.57 us
    add x1, other arithmetic, shards(): small = small + jnp.pad(part, ((at, total - at - rows), (0, lat - width)))  1.14 us
  transfers between devices with their start and end apart: 2, of which 0 were waited for; matrix products, arithmetic and copies ran while one was open for 0% of the time, Pallas kernels for 39%

profile of v2, /device:TPU:0, one launch (start us, length us, event | category | flops | bytes accessed | tf_op | source)
XLA Modules:
  0.0 29.7 jit_solution(3909601049723118346)
XLA Ops:
  0.0 0.0 copy-start
  0.0 1.1 %pad_add_fusion.small.refs_1_.refs_2_ = f32[392,256]{1,0:T(8,128)S(1)} fusion(f32[1,96]{1,0:T(1,128)} %bitcast.1, f32[96,96]{1,0:T(8,128)} %param.9, f32[96,96]{1,0:T(8,128)} %param.8, f32[64,256]{1,0:T(8,128)} %param.13, f32[64,256]{1,0:T(8,128)} %param.12, f32[64,256]{1,0:T(8,128)} %param.11), kind=kLoop, calls=%fused_computation | loop fusion | flops 501760 | bytes 672128 | tf_op jit(solution)/shard_map/add | solution.py:490
  1.1 0.2 prepare.1
  1.4 1.6 %copy-done = f32[96,64,256]{2,1,0:T(8,128)S(1)} copy-done((f32[96,64,256]{2,1,0:T(8,128)S(1)}, f32[96,64,256]{2,1,0:T(8,128)}, u32[]{:S(2)}) %copy-start) | copy-done | bytes 6291480
  2.9 6.9 %interior.2 = (f32[4,2,96,256]{3,2,1,0:T(8,128)S(1)}, f32[4,104,256]{2,1,0:T(8,128)S(1)}, f32[4,104,256]{2,1,0:T(8,128)S(1)}, f32[13,96,256]{2,1,0:T(8,128)S(1)}...) custom-call(f32[96,64,256]{2,1,0:T(8,128)S(1)} %copy-done, ...), custom_call_target="tpu_custom_call" | custom-call | tf_op jit(solution)/shard_map/interior/pallas_call | solution.py:450
  9.9 0.5 %collective-permute-start = (f32[4,104,256]{2,1,0:T(8,128)S(1)}, f32[4,104,256]{2,1,0:T(8,128)S(1)}, u32[]{:S(2)}, u32[]{:S(2)}) collective-permute-start(f32[4,104,256]{2,1,0:T(8,128)S(1)} %get-tuple-element.23), channel_id=1, source_target_pairs={{0,1},{1,0},{2,3},{3,2},{4,5},{5,4},{6,7},{7,6},{8,9},{9,8},{10,11... | collective-permute-start | bytes 1277960 | tf_op jit(solution)/shard_map/ppermute | solution.py:495
  10.4 3.5 %collective-permute-start.1 = (f32[4,104,256]{2,1,0:T(8,128)S(1)}, f32[4,104,256]{2,1,0:T(8,128)S(1)}, u32[]{:S(2)}, u32[]{:S(2)}) collective-permute-start(f32[4,104,256]{2,1,0:T(8,128)S(1)} %get-tuple-element.24), channel_id=1, source_target_pairs={{0,15},{1,2},{2,1},{3,4},{4,3},{5,6},{6,5},{7,8},{8,7},{9,10},{10,... | collective-permute-start | bytes 1277960 | tf_op jit(solution)/shard_map/ppermute | solution.py:496
  13.9 11.6 %interior.3 = (f32[96,64,256]{2,1,0:T(8,128)}, f32[2,2,96,8,128]{4,3,2,1,0:T(8,128)S(1)}, f32[4,2,96,256]{3,2,1,0:T(8,128)S(1)}) custom-call(f32[5,96,128]{2,1,0:T(8,128)S(1)} %get-tuple-element.19.refs_2_.refs_0_.refs_3_, bf16[96,288]{1,0:T(8,128)(2,1)S(1)} %get-tuple-element.20.refs_3_.refs_1_.refs_4_, ...), custom_call_target="tpu_custom_call" | custom-call | tf_op jit(solution)/shard_map/interior/pallas_call | solution.py:450
  25.5 0.0 collective-permute-done.refs_0_
  25.5 0.0 collective-permute-done.1.refs_1_
  25.5 4.2 %edges.1 = f32[96,64,256]{2,1,0:T(8,128)} custom-call(f32[4,104,256]{2,1,0:T(8,128)S(1)} %collective-permute-done.refs_0_, f32[4,104,256]{2,1,0:T(8,128)S(1)} %collective-permute-done.1.refs_1_, f32[392,256]{1,0:T(8,128)S(1)} %pad_add_fusion.small.refs_1_.refs_2_, ...), custom_call_target="tpu_custom_call", output_to_operand_aliasing={{}: (10, {})} | custom-call | tf_op jit(solution)/shard_map/edges/pallas_call | solution.py:463
Async XLA Ops:
  0.0 2.9 %copy-start = (f32[96,64,256]{2,1,0:T(8,128)S(1)}, f32[96,64,256]{2,1,0:T(8,128)}, u32[]{:S(2)}) copy-start(f32[96,64,256]{2,1,0:T(8,128)} %refs_0_.1) | copy-start | bytes 18874372
  9.9 15.6 %collective-permute-start = (f32[4,104,256]{2,1,0:T(8,128)S(1)}, f32[4,104,256]{2,1,0:T(8,128)S(1)}, u32[]{:S(2)}, u32[]{:S(2)}) collective-permute-start(f32[4,104,256]{2,1,0:T(8,128)S(1)} %get-tuple-element.23), channel_id=1, source_target_pairs={{0,1},{1,0},{2,3},{3,2},{4,5},{5,4},{6,7},{7,6},{8,9},{9,8},{10,11... | collective-permute-start | bytes 1277960 | tf_op jit(solution)/shard_map/ppermute | solution.py:495
  10.4 15.1 %collective-permute-start.1 = (f32[4,104,256]{2,1,0:T(8,128)S(1)}, f32[4,104,256]{2,1,0:T(8,128)S(1)}, u32[]{:S(2)}, u32[]{:S(2)}) collective-permute-start(f32[4,104,256]{2,1,0:T(8,128)S(1)} %get-tuple-element.24), channel_id=1, source_target_pairs={{0,15},{1,2},{2,1},{3,4},{4,3},{5,6},{6,5},{7,8},{8,7},{9,10},{10,... | collective-permute-start | bytes 1277960 | tf_op jit(solution)/shard_map/ppermute | solution.py:496

commit v3 on v2

--- a/solution.py
+++ b/solution.py
@@ -179,7 +179,9 @@
     refs = list(refs)
     take = lambda n: [refs.pop(0) for _ in range(n)]
     blocks = lon // 8
-    stop = jnp.where(lax.axis_index("lon") < 2, late, early)
+    begins = lax.axis_index("lon") < 2
+    extra = begins & (lax.axis_index("parts") == 0)
+    stop = jnp.where(begins, late, early)
     if first:
         x_ref, small, cols, ws, wa, co = take(6)
         save_ref, near, far, carried, cbuf, obuf, zbuf = take(7)
@@ -268,6 +270,14 @@
                 continue
             store_z(rows, add_scaled(operate(at(d2, 0), at(ww, 0), w, at(ww, 3), c4), cols[4, rows, :], old))
 
+    def half(begin):
+        if first:
+            wait(fetch(stop + 1))
+        for s in range(begin, begin + 4):
+            advance(stop, s, 4)
+        if not first:
+            start(flush(obuf, stop - 1))
+
     def body(t, _):
         if first:
 
@@ -299,12 +309,13 @@
         save_ref[3, 0] = ww[3]
         save_ref[3, 1] = ww[0]
         lax.fori_loop(1, stop, body, 0)
+        pl.when(extra)(functools.partial(half, 0))
         n = 0
         for name, slots in RESUME:
             for slot in slots:
                 carried[n] = rings[name][slot]
                 n += 1
-        lax.fori_loop(stop + 1, blocks, lambda b, _: (wait(fetch(b)), 0)[1], 0)
+        lax.fori_loop(jnp.where(extra, stop + 2, stop + 1), blocks, lambda b, _: (wait(fetch(b)), 0)[1], 0)
         even = lax.rem(lax.axis_index("lon"), 2) == 0
         for msg_ref, east in ((near, even), (far, jnp.logical_not(even))):
             block, row = jnp.where(east, blocks - 1, 0), jnp.where(east, 4, 0)
@@ -314,7 +325,8 @@
                 for f in range(3):
                     msg_ref[j, pl.ds(levels + f, 1), :] = small[pl.ds(f * lon + at + j, 1), :]
     else:
-        lax.fori_loop(stop, blocks, body, 0)
+        pl.when(extra)(functools.partial(half, 4))
+        lax.fori_loop(jnp.where(extra, stop + 1, stop), blocks, body, 0)
         finish(lon - 5)
         edge_ref[0] = obuf[blocks - 2]
         edge_ref[1] = obuf[blocks - 1]
@@ -436,7 +448,7 @@
     saved = shape(4, 2, levels, lat)
     if first:
         outs = [saved, shape(4, levels + 8, lat), shape(4, levels + 8, lat),
-                shape(CARRIED, levels, lat), shape(blocks + 1, 2, levels, 8, H), shape(LATE, 2, levels, 8, H),
+                shape(CARRIED, levels, lat), shape(blocks + 1, 2, levels, 8, H), shape(LATE + 1, 2, levels, 8, H),
                 shape(3 * levels, lat, dtype=BF16)]
         in_specs = [HBM] + [VM] * 5
         out_specs = [VM] * len(outs)
@@ -445,7 +457,7 @@
         outs = [shape(levels, lon, lat), shape(2, 2, levels, 8, H), saved]
         in_specs = [VM] * 8
         out_specs = [HBM, VM, VM]
-        scratch = [pltpu.VMEM((blocks, 2, levels, 8, H), F32), pltpu.VMEM((3 * levels, lat), BF16),
+        scratch = [pltpu.VMEM((blocks + 1, 2, levels, 8, H), F32), pltpu.VMEM((3 * levels, lat), BF16),
                    pltpu.SemaphoreType.DMA((2, blocks))]
     return pl.pallas_call(
         functools.partial(interior, first, EARLY, LATE, levels, lon),

time: 29.8 us -> 28.4 us (0.953)
  starting transfers between devices: 4.04 us -> 3.05 us
  Pallas kernels: 22.9 us -> 22.4 us
    ppermute x1, starting transfers between devices: 3.53 us -> 2.53 us  [shards(): lax.ppermute(far, 'lon', [(i, (i + 2 * (i % 2) - 1) % count) for i in ran...]
    pallas_call x2, Pallas kernels: 18.5 us -> 18.1 us  [run_interior(): pl.pallas_call(functools.partial(interior, first, EARLY, LATE, levels, lo...]
  transfers between devices with their start and end apart: 2 -> 2, of which waited for: 0 -> 0; matrix products, arithmetic and copies ran while one was open for 0% -> 0% of each run, Pallas kernels for 39% -> 36%
where the time goes in v3:
time: 28.4 us; the launch traced here: 28.2 us
  Pallas kernels  22.4 us (79%)
  starting transfers between devices  3.05 us (11%)
  local copies, waits for them, and re-layouts  1.57 us (6%)
  other arithmetic  1.14 us (4%)
    pallas_call x2, Pallas kernels, run_interior(): pl.pallas_call(functools.partial(interior, first, EARLY, LATE, levels, lo...  18.1 us
    pallas_call x1, Pallas kernels, run_edges(): pl.pallas_call(functools.partial(edges, levels, lon), out_shape=shape(lev...  4.11 us
    ppermute x1, starting transfers between devices, shards(): lax.ppermute(far, 'lon', [(i, (i + 2 * (i % 2) - 1) % count) for i in ran...  2.53 us
    unnamed x2, local copies, waits for them, and re-layouts  1.57 us
    add x1, other arithmetic, shards(): small = small + jnp.pad(part, ((at, total - at - rows), (0, lat - width)))  1.14 us
  transfers between devices with their start and end apart: 2, of which 0 were waited for; matrix products, arithmetic and copies ran while one was open for 0% of the time, Pallas kernels for 36%

profile of v3, /device:TPU:0, one launch (start us, length us, event | category | flops | bytes accessed | tf_op | source)
XLA Modules:
  0.0 28.2 jit_solution(7052447684950837623)
XLA Ops:
  0.0 0.0 copy-start
  0.0 1.1 %pad_add_fusion.small.refs_1_.refs_2_ = f32[392,256]{1,0:T(8,128)S(1)} fusion(f32[1,96]{1,0:T(1,128)} %bitcast.1, f32[96,96]{1,0:T(8,128)} %param.9, f32[96,96]{1,0:T(8,128)} %param.8, f32[64,256]{1,0:T(8,128)} %param.13, f32[64,256]{1,0:T(8,128)} %param.12, f32[64,256]{1,0:T(8,128)} %param.11), kind=kLoop, calls=%fused_computation | loop fusion | flops 501760 | bytes 672128 | tf_op jit(solution)/shard_map/add | solution.py:502
  1.1 0.2 prepare.1
  1.4 1.6 %copy-done = f32[96,64,256]{2,1,0:T(8,128)S(1)} copy-done((f32[96,64,256]{2,1,0:T(8,128)S(1)}, f32[96,64,256]{2,1,0:T(8,128)}, u32[]{:S(2)}) %copy-start) | copy-done | bytes 6291480
  2.9 7.9 %interior.2 = (f32[4,2,96,256]{3,2,1,0:T(8,128)S(1)}, f32[4,104,256]{2,1,0:T(8,128)S(1)}, f32[4,104,256]{2,1,0:T(8,128)S(1)}, f32[13,96,256]{2,1,0:T(8,128)S(1)}...) custom-call(f32[96,64,256]{2,1,0:T(8,128)S(1)} %copy-done, ...), custom_call_target="tpu_custom_call" | custom-call | tf_op jit(solution)/shard_map/interior/pallas_call | solution.py:462
  10.8 0.5 %collective-permute-start = (f32[4,104,256]{2,1,0:T(8,128)S(1)}, f32[4,104,256]{2,1,0:T(8,128)S(1)}, u32[]{:S(2)}, u32[]{:S(2)}) collective-permute-start(f32[4,104,256]{2,1,0:T(8,128)S(1)} %get-tuple-element.23), channel_id=1, source_target_pairs={{0,1},{1,0},{2,3},{3,2},{4,5},{5,4},{6,7},{7,6},{8,9},{9,8},{10,11... | collective-permute-start | bytes 1277960 | tf_op jit(solution)/shard_map/ppermute | solution.py:507
  11.3 2.5 %collective-permute-start.1 = (f32[4,104,256]{2,1,0:T(8,128)S(1)}, f32[4,104,256]{2,1,0:T(8,128)S(1)}, u32[]{:S(2)}, u32[]{:S(2)}) collective-permute-start(f32[4,104,256]{2,1,0:T(8,128)S(1)} %get-tuple-element.24), channel_id=1, source_target_pairs={{0,15},{1,2},{2,1},{3,4},{4,3},{5,6},{6,5},{7,8},{8,7},{9,10},{10,... | collective-permute-start | bytes 1277960 | tf_op jit(solution)/shard_map/ppermute | solution.py:508
  13.9 10.2 %interior.3 = (f32[96,64,256]{2,1,0:T(8,128)}, f32[2,2,96,8,128]{4,3,2,1,0:T(8,128)S(1)}, f32[4,2,96,256]{3,2,1,0:T(8,128)S(1)}) custom-call(f32[5,96,128]{2,1,0:T(8,128)S(1)} %get-tuple-element.19.refs_2_.refs_0_.refs_3_, bf16[96,288]{1,0:T(8,128)(2,1)S(1)} %get-tuple-element.20.refs_3_.refs_1_.refs_4_, ...), custom_call_target="tpu_custom_call" | custom-call | tf_op jit(solution)/shard_map/interior/pallas_call | solution.py:462
  24.1 0.0 collective-permute-done.refs_0_
  24.1 0.0 collective-permute-done.1.refs_1_
  24.1 4.1 %edges.1 = f32[96,64,256]{2,1,0:T(8,128)} custom-call(f32[4,104,256]{2,1,0:T(8,128)S(1)} %collective-permute-done.refs_0_, f32[4,104,256]{2,1,0:T(8,128)S(1)} %collective-permute-done.1.refs_1_, f32[392,256]{1,0:T(8,128)S(1)} %pad_add_fusion.small.refs_1_.refs_2_, ...), custom_call_target="tpu_custom_call", output_to_operand_aliasing={{}: (10, {})} | custom-call | tf_op jit(solution)/shard_map/edges/pallas_call | solution.py:475
Async XLA Ops:
  0.0 2.9 %copy-start = (f32[96,64,256]{2,1,0:T(8,128)S(1)}, f32[96,64,256]{2,1,0:T(8,128)}, u32[]{:S(2)}) copy-start(f32[96,64,256]{2,1,0:T(8,128)} %refs_0_.1) | copy-start | bytes 18874372
  10.8 13.3 %collective-permute-start = (f32[4,104,256]{2,1,0:T(8,128)S(1)}, f32[4,104,256]{2,1,0:T(8,128)S(1)}, u32[]{:S(2)}, u32[]{:S(2)}) collective-permute-start(f32[4,104,256]{2,1,0:T(8,128)S(1)} %get-tuple-element.23), channel_id=1, source_target_pairs={{0,1},{1,0},{2,3},{3,2},{4,5},{5,4},{6,7},{7,6},{8,9},{9,8},{10,11... | collective-permute-start | bytes 1277960 | tf_op jit(solution)/shard_map/ppermute | solution.py:507
  11.3 12.8 %collective-permute-start.1 = (f32[4,104,256]{2,1,0:T(8,128)S(1)}, f32[4,104,256]{2,1,0:T(8,128)S(1)}, u32[]{:S(2)}, u32[]{:S(2)}) collective-permute-start(f32[4,104,256]{2,1,0:T(8,128)S(1)} %get-tuple-element.24), channel_id=1, source_target_pairs={{0,15},{1,2},{2,1},{3,4},{4,3},{5,6},{6,5},{7,8},{8,7},{9,10},{10,... | collective-permute-start | bytes 1277960 | tf_op jit(solution)/shard_map/ppermute | solution.py:508

commit v4 on v3

--- a/solution.py
+++ b/solution.py
@@ -184,21 +184,18 @@
     stop = jnp.where(begins, late, early)
     if first:
         x_ref, small, cols, ws, wa, co = take(6)
-        save_ref, near, far, carried, cbuf, obuf, zbuf = take(7)
-        (in_sem,) = take(1)
+        save_ref, near, far, carried, obuf, zbuf = take(6)
     else:
-        cols, ws, wa, co, carried, cbuf, done, z_in = take(8)
+        x_ref, cols, ws, wa, co, carried, done, z_in = take(8)
         out_ref, edge_ref, save_ref = take(3)
         obuf, zbuf, out_sem = take(3)
-    rr, uu, yy, ww, d1, d2 = take(6)
+    cbuf, rr, uu, yy, ww, d1, d2 = take(7)
     assert not refs
     rings = {"r": rr, "u": uu, "y": yy, "w": ww, "d1": d1, "d2": d2}
 
-    def fetch(b):
-        return [
-            pltpu.make_async_copy(x_ref.at[:, pl.ds(8 * b, 8), pl.ds(h * H, H)], cbuf.at[b, h], in_sem.at[h, b])
-            for h in range(2)
-        ]
+    def bring(b):
+        for h in range(2):
+            cbuf[0, h] = x_ref[:, b, h]
 
     def flush(src, b):
         return [
@@ -206,14 +203,10 @@
             for h in range(2)
         ]
 
-    if first:
-        for b in range(blocks):
-            start(fetch(b))
-
+    bring(0 if first else stop)
     rows_in = cbuf.reshape(cbuf.shape[0] * 2 * levels * 8, H)
     rows_out = obuf.reshape(obuf.shape[0] * 2 * levels * 8, H)
     if first:
-        wait(fetch(0))
         rr[0] = mix(ws[...], load_row(rows_in, 0, 0, levels))
         save_ref[0, 0] = rr[0]
     else:
@@ -245,7 +238,9 @@
         q = lambda n: (s + n) % 4
         if stages == 4:
             finish(i - 5)
-        rr[(s + 1) % 4] = mix(ws[...], load_row(rows_in, t + (s + 1) // 8, (s + 1) % 8, levels))
+        if s == 7:
+            bring(jnp.minimum(t + 1, blocks - 1))
+        rr[(s + 1) % 4] = mix(ws[...], load_row(rows_in, 0, (s + 1) % 8, levels))
         if not stages:
             return
         for rows in groups(levels):
@@ -271,20 +266,12 @@
             store_z(rows, add_scaled(operate(at(d2, 0), at(ww, 0), w, at(ww, 3), c4), cols[4, rows, :], old))
 
     def half(begin):
-        if first:
-            wait(fetch(stop + 1))
         for s in range(begin, begin + 4):
             advance(stop, s, 4)
         if not first:
             start(flush(obuf, stop - 1))
 
     def body(t, _):
-        if first:
-
-            @pl.when(t + 1 < blocks)
-            def _():
-                wait(fetch(t + 1))
-
         for s in range(8):
             advance(t, s, 4)
 
@@ -297,7 +284,6 @@
         return 0
 
     if first:
-        wait(fetch(1))
         for s in range(8):
             advance(0, s, s // 2)
             if s == 3:
@@ -315,13 +301,13 @@
             for slot in slots:
                 carried[n] = rings[name][slot]
                 n += 1
-        lax.fori_loop(jnp.where(extra, stop + 2, stop + 1), blocks, lambda b, _: (wait(fetch(b)), 0)[1], 0)
         even = lax.rem(lax.axis_index("lon"), 2) == 0
         for msg_ref, east in ((near, even), (far, jnp.logical_not(even))):
             block, row = jnp.where(east, blocks - 1, 0), jnp.where(east, 4, 0)
             at = jnp.where(east, lon - 4, 0)
+            bring(block)
             for j in range(4):
-                msg_ref[j, :levels, :] = load_row(rows_in, block, row + j, levels)
+                msg_ref[j, :levels, :] = load_row(rows_in, 0, row + j, levels)
                 for f in range(3):
                     msg_ref[j, pl.ds(levels + f, 1), :] = small[pl.ds(f * lon + at + j, 1), :]
     else:
@@ -390,8 +376,9 @@
             n = w0 + j
             step3(levels, c, base + n, (y, n), (y, n + 1), (y, n - 1), (g, n), (w, n + 1))
         ob = obuf.at[side]
-        ob[...] = edge[...]
-        flat = ob.reshape(2 * levels * 8, H)
+        for h in range(2):
+            ob[h] = edge[h]
+        flat = ob.reshape(3 * levels * 8, H)
         for j in range(4):
             n = z0 + j
             z = zbuf.at[side, j]
@@ -448,11 +435,11 @@
     saved = shape(4, 2, levels, lat)
     if first:
         outs = [saved, shape(4, levels + 8, lat), shape(4, levels + 8, lat),
-                shape(CARRIED, levels, lat), shape(blocks + 1, 2, levels, 8, H), shape(LATE + 1, 2, levels, 8, H),
+                shape(CARRIED, levels, lat), shape(LATE + 1, 2, levels, 8, H),
                 shape(3 * levels, lat, dtype=BF16)]
-        in_specs = [HBM] + [VM] * 5
+        in_specs = [VM] * 6
         out_specs = [VM] * len(outs)
-        scratch = [pltpu.SemaphoreType.DMA((2, blocks))]
+        scratch = []
     else:
         outs = [shape(levels, lon, lat), shape(2, 2, levels, 8, H), saved]
         in_specs = [VM] * 8
@@ -464,7 +451,7 @@
         out_shape=outs,
         in_specs=in_specs,
         out_specs=out_specs,
-        scratch_shapes=scratch + [ring, ring, ring, ring, ring, ring],
+        scratch_shapes=scratch + [pltpu.VMEM((2, 2, levels, 8, H), F32), ring, ring, ring, ring, ring, ring],
         compiler_params=params(LIM_A if first else LIM_B),
         name="interior",
     )(*operands)
@@ -482,7 +469,7 @@
             pltpu.VMEM((2, 5, 24, lat), F32),
             window(8), window(8), window(8), window(10), window(8), window(8),
             pltpu.VMEM((2, 4, 3 * levels, lat), BF16),
-            pltpu.VMEM((2, 2, levels, 8, H), F32),
+            pltpu.VMEM((2, 3, levels, 8, H), F32),
             pltpu.VMEM((2, 4, levels + 8, lat), F32),
             pltpu.SemaphoreType.DMA((3, 2)),
         ],
@@ -502,12 +489,13 @@
         small = small + jnp.pad(part, ((at, total - at - rows), (0, lat - width)))
         at += rows
     cols, ws, wa, co = run_prepare(levels, lon, lat, small)
-    save_l, near, far, carried, blocks_in, blocks_out, z = run_interior(
-        True, levels, lon, lat, (cotangent, small, cols, ws, wa, co))
+    tiles = cotangent.reshape(levels, lon // 8, 8, 2, H).transpose(0, 1, 3, 2, 4)
+    save_l, near, far, carried, blocks_out, z = run_interior(
+        True, levels, lon, lat, (tiles, small, cols, ws, wa, co))
     near = lax.ppermute(near, "lon", [(i, i ^ 1) for i in range(count)])
     far = lax.ppermute(far, "lon", [(i, (i + 2 * (i % 2) - 1) % count) for i in range(count)])
     out, edge_r, save_r = run_interior(
-        False, levels, lon, lat, (cols, ws, wa, co, carried, blocks_in, blocks_out, z))
+        False, levels, lon, lat, (tiles, cols, ws, wa, co, carried, blocks_out, z))
     return run_edges(levels, lon, lat, (near, far, small, cols, ws, wa, save_l, save_r, blocks_out, edge_r, out))
 
 

time: 28.4 us -> 27.8 us (0.979)
  Pallas kernels: 22.4 us -> 22.1 us
    pallas_call x2, Pallas kernels: 18.1 us -> 17.7 us  [run_interior(): pl.pallas_call(functools.partial(interior, first, EARLY, LATE, levels, lo...]
  transfers between devices with their start and end apart: 2 -> 2, of which waited for: 0 -> 0; matrix products, arithmetic and copies ran while one was open for 0% -> 0% of each run, Pallas kernels for 36% -> 38%
where the time goes in v4:
time: 27.8 us; the launch traced here: 27.6 us
  Pallas kernels  22.1 us (79%)
  starting transfers between devices  2.78 us (10%)
  local copies, waits for them, and re-layouts  1.57 us (6%)
  other arithmetic  1.14 us (4%)
    pallas_call x2, Pallas kernels, run_interior(): pl.pallas_call(functools.partial(interior, first, EARLY, LATE, levels, lo...  17.7 us
    pallas_call x1, Pallas kernels, run_edges(): pl.pallas_call(functools.partial(edges, levels, lon), out_shape=shape(lev...  4.16 us
    ppermute x1, starting transfers between devices, shards(): lax.ppermute(far, 'lon', [(i, (i + 2 * (i % 2) - 1) % count) for i in ran...  2.26 us
    unnamed x2, local copies, waits for them, and re-layouts  1.57 us
    add x1, other arithmetic, shards(): small = small + jnp.pad(part, ((at, total - at - rows), (0, lat - width)))  1.14 us
  transfers between devices with their start and end apart: 2, of which 0 were waited for; matrix products, arithmetic and copies ran while one was open for 0% of the time, Pallas kernels for 38%

profile of v4, /device:TPU:0, one launch (start us, length us, event | category | flops | bytes accessed | tf_op | source)
XLA Modules:
  0.0 27.6 jit_solution(7657913020908030905)
XLA Ops:
  0.0 0.0 copy-start
  0.0 1.1 %pad_add_fusion.small.refs_1_.refs_2_ = f32[392,256]{1,0:T(8,128)S(1)} fusion(f32[1,96]{1,0:T(1,128)} %bitcast.6, f32[96,96]{1,0:T(8,128)} %param.9, f32[96,96]{1,0:T(8,128)} %param.8, f32[64,256]{1,0:T(8,128)} %param.13, f32[64,256]{1,0:T(8,128)} %param.12, f32[64,256]{1,0:T(8,128)} %param.11), kind=kLoop, calls=%fused_computation | loop fusion | flops 501760 | bytes 672128 | tf_op jit(solution)/shard_map/add | solution.py:489
  1.1 0.2 prepare.1
  1.4 1.6 %copy-done = f32[96,64,256]{2,1,0:T(8,128)S(1)} copy-done((f32[96,64,256]{2,1,0:T(8,128)S(1)}, f32[96,64,256]{2,1,0:T(8,128)}, u32[]{:S(2)}) %copy-start) | copy-done | bytes 6291480
  2.9 7.2 %interior.2 = (f32[4,2,96,256]{3,2,1,0:T(8,128)S(1)}, f32[4,104,256]{2,1,0:T(8,128)S(1)}, f32[4,104,256]{2,1,0:T(8,128)S(1)}, f32[13,96,256]{2,1,0:T(8,128)S(1)}...) custom-call(f32[96,8,2,8,128]{4,3,2,1,0:T(8,128)S(1)} %bitcast.4, ...), custom_call_target="tpu_custom_call" | custom-call | tf_op jit(solution)/shard_map/interior/pallas_call | solution.py:449
  10.1 0.5 %collective-permute-start = (f32[4,104,256]{2,1,0:T(8,128)S(1)}, f32[4,104,256]{2,1,0:T(8,128)S(1)}, u32[]{:S(2)}, u32[]{:S(2)}) collective-permute-start(f32[4,104,256]{2,1,0:T(8,128)S(1)} %get-tuple-element.22), channel_id=1, source_target_pairs={{0,1},{1,0},{2,3},{3,2},{4,5},{5,4},{6,7},{7,6},{8,9},{9,8},{10,11... | collective-permute-start | bytes 1277960 | tf_op jit(solution)/shard_map/ppermute | solution.py:495
  10.6 2.3 %collective-permute-start.1 = (f32[4,104,256]{2,1,0:T(8,128)S(1)}, f32[4,104,256]{2,1,0:T(8,128)S(1)}, u32[]{:S(2)}, u32[]{:S(2)}) collective-permute-start(f32[4,104,256]{2,1,0:T(8,128)S(1)} %get-tuple-element.23), channel_id=1, source_target_pairs={{0,15},{1,2},{2,1},{3,4},{4,3},{5,6},{6,5},{7,8},{8,7},{9,10},{10,... | collective-permute-start | bytes 1277960 | tf_op jit(solution)/shard_map/ppermute | solution.py:496
  12.9 10.6 %interior.3 = (f32[96,64,256]{2,1,0:T(8,128)}, f32[2,2,96,8,128]{4,3,2,1,0:T(8,128)S(1)}, f32[4,2,96,256]{3,2,1,0:T(8,128)S(1)}) custom-call(f32[96,8,2,8,128]{4,3,2,1,0:T(8,128)S(1)} %bitcast.5, f32[5,96,128]{2,1,0:T(8,128)S(1)} %get-tuple-element.18.refs_2_.refs_1_.refs_3_, bf16[96,288]{1,0:T(8,128)(2,1)S(1)} %get-tuple-element.19.refs_3_.refs_2_.refs_4_, ...), custom_call_target="tpu_custom_call" | custom-call | tf_op jit(solution)/shard_map/interior/pallas_call | solution.py:449
  23.5 0.0 collective-permute-done.refs_0_
  23.5 0.0 collective-permute-done.1.refs_1_
  23.5 4.2 %edges.1 = f32[96,64,256]{2,1,0:T(8,128)} custom-call(f32[4,104,256]{2,1,0:T(8,128)S(1)} %collective-permute-done.refs_0_, f32[4,104,256]{2,1,0:T(8,128)S(1)} %collective-permute-done.1.refs_1_, f32[392,256]{1,0:T(8,128)S(1)} %pad_add_fusion.small.refs_1_.refs_2_, ...), custom_call_target="tpu_custom_call", output_to_operand_aliasing={{}: (10, {})} | custom-call | tf_op jit(solution)/shard_map/edges/pallas_call | solution.py:462
Async XLA Ops:
  0.0 2.9 %copy-start = (f32[96,64,256]{2,1,0:T(8,128)S(1)}, f32[96,64,256]{2,1,0:T(8,128)}, u32[]{:S(2)}) copy-start(f32[96,64,256]{2,1,0:T(8,128)} %param.7) | copy-start | bytes 18874372
  10.1 13.4 %collective-permute-start = (f32[4,104,256]{2,1,0:T(8,128)S(1)}, f32[4,104,256]{2,1,0:T(8,128)S(1)}, u32[]{:S(2)}, u32[]{:S(2)}) collective-permute-start(f32[4,104,256]{2,1,0:T(8,128)S(1)} %get-tuple-element.22), channel_id=1, source_target_pairs={{0,1},{1,0},{2,3},{3,2},{4,5},{5,4},{6,7},{7,6},{8,9},{9,8},{10,11... | collective-permute-start | bytes 1277960 | tf_op jit(solution)/shard_map/ppermute | solution.py:495
  10.6 12.8 %collective-permute-start.1 = (f32[4,104,256]{2,1,0:T(8,128)S(1)}, f32[4,104,256]{2,1,0:T(8,128)S(1)}, u32[]{:S(2)}, u32[]{:S(2)}) collective-permute-start(f32[4,104,256]{2,1,0:T(8,128)S(1)} %get-tuple-element.23), channel_id=1, source_target_pairs={{0,15},{1,2},{2,1},{3,4},{4,3},{5,6},{6,5},{7,8},{8,7},{9,10},{10,... | collective-permute-start | bytes 1277960 | tf_op jit(solution)/shard_map/ppermute | solution.py:496
